TPU v7x, 32 devices: a whole 2x2x4 slice. The times are simulated.
32 devices in a mesh: slab: 8 (over z, x), mp: 4 (over y, core).
Axes of the slice: x: 2, y: 2, z: 4, core: 2. Of those that a mesh axis runs over, the one named last changes fastest.
Arguments:
- feats: float32 [56, 28, 7, 384], P('slab', 'mp'), may hold values from -6 to 6
- labels: int32 [56, 28, 7], P('slab', 'mp'), may hold values from 0 to 13
- valid: int32 [56, 28, 7], P('slab', 'mp'), may hold values from 0 to 1, as said below
- params: float32 [872558], replicated
- moment_one: float32 [872558], replicated, may hold values from -1.5258789e-05 to 1.5258789e-05
- moment_two: float32 [872558], replicated, may hold values from 1.1460556e-13 to 4.5842225e-13
Outputs:
- loss_sum: float32 [], replicated
- valid_count: float32 [], replicated
- grad_norm: float32 [], replicated
- new_params: float32 [872558], replicated
- new_first: float32 [872558], replicated
- new_second: float32 [872558], replicated
Inputs may be any that keep to these rules, and one draw needn't show every extreme that they name: valid is 0 or 1; the share of ones rises with depth.
All inputs are finite; a program needn't handle non-finite values.
Results may differ from a plain program's by a relative error of at most 0.0003.
Values sent between devices are 32-bit elements; how exact they have to be, the bound alone decides.
No kernel may reach another device: no remote copies, remote signals or barrier semaphores. Data moves between devices by JAX's collectives and lax.ppermute only.
A program may use at most 192 MiB of HBM per device.

v0:
```python
import math

import jax
import jax.numpy as jnp
from jax import lax
from jax.sharding import PartitionSpec as P

EMB = 96
HEADS = 6
HDIM = 16
HID = 384
MERGE = 384
CLASSES = 14
WIN = 7
SHIFT = 3
LAYERS = 3
STEP = 10


HIGH = lax.Precision.HIGHEST
eps_norm = 1e-05
beta_one = 0.9
beta_two = 0.999
adam_eps = 1e-08
learn_rate = 0.05
decay_rate = 0.05
clip_norm = 0.01


def extended(cells, sides, width):
    for axis, dim in sides:
        count = lax.axis_size(axis)
        ends = count - 1
        head = lax.slice_in_dim(cells, 0, width, axis=dim)
        tail = lax.slice_in_dim(cells, cells.shape[dim] - width, cells.shape[dim], axis=dim)
        cells = jnp.concatenate(
            [
                lax.ppermute(tail, axis, [(i, (i + 1) % count) for i in range(ends)]),
                cells,
                lax.ppermute(head, axis, [((i + 1) % count, i) for i in range(ends)]),
            ],
            axis=dim,
        )
    return cells


def passed_along(value, axis, steps):
    count = lax.axis_size(axis)
    pairs = [(source, (source + steps) % count) for source in range(count)]
    return lax.ppermute(value, axis, pairs)


def layout():
    table = [
        ("merge_gain", (MERGE,), 0, 1),
        ("merge_bias", (MERGE,), 1, 1),
        ("merge_weight", (MERGE, EMB), 2, MERGE),
    ]
    for layer in range(LAYERS):
        tag = str(layer)
        table += [
            ("first_gain" + tag, (EMB,), 0, 1),
            ("first_bias" + tag, (EMB,), 1, 1),
            ("second_gain" + tag, (EMB,), 0, 1),
            ("second_bias" + tag, (EMB,), 1, 1),
            ("qkv_weight" + tag, (EMB, 3 * EMB), 2, EMB),
            ("qkv_bias" + tag, (3 * EMB,), 1, 1),
            ("proj_weight" + tag, (EMB, EMB), 2, EMB // 4),
            ("proj_bias" + tag, (EMB,), 1, 1),
            ("hidden_weight" + tag, (EMB, HID), 2, EMB),
            ("hidden_bias" + tag, (HID,), 1, 1),
            ("output_weight" + tag, (HID, EMB), 2, HID),
            ("output_bias" + tag, (EMB,), 1, 1),
        ]
    table += [
        ("conv_weight0", (3, 3, 3, EMB, EMB), 2, 27 * EMB),
        ("conv_bias0", (EMB,), 1, 1),
        ("conv_weight1", (3, 3, 3, EMB, EMB), 2, 27 * EMB),
        ("conv_bias1", (EMB,), 1, 1),
    ]
    table += [
        ("inorm_gain", (EMB,), 0, 1),
        ("inorm_bias", (EMB,), 1, 1),
        ("head_weight", (EMB, CLASSES), 2, EMB),
        ("head_bias", (CLASSES,), 1, 1),
    ]
    return table


def carve(flat):
    parts = {}
    offset = 0
    for name, shape, kind, fan in layout():
        count = math.prod(shape)
        parts[name] = flat[offset : offset + count].reshape(shape)
        offset += count
    return parts


def norm_rows(tokens, gain_row, bias_row):
    average = jnp.mean(tokens, -1, keepdims=True)
    centred = tokens - average
    spread = jnp.mean(centred * centred, -1, keepdims=True)
    return centred * lax.rsqrt(spread + eps_norm) * gain_row + bias_row


def matmul(tokens, weight):
    return jnp.einsum("...c,cd->...d", tokens, weight, precision=HIGH)


def embed(parts, feats):
    return matmul(norm_rows(feats, parts["merge_gain"], parts["merge_bias"]), parts["merge_weight"])


def conv_valid(padded, weight):
    planes, height, breadth = (padded.shape[0] - 2, padded.shape[1] - 2, padded.shape[2] - 2)
    total = jnp.zeros((planes, height, breadth, weight.shape[-1]), jnp.float32)
    for first in range(3):
        for second in range(3):
            for third in range(3):
                total = total + matmul(
                    padded[
                        first : first + planes, second : second + height, third : third + breadth
                    ],
                    weight[first, second, third],
                )
    return total


def rim_forward(volume):
    grown = extended(volume, (("slab", 0), ("mp", 1)), 1)
    return jnp.pad(grown, ((0, 0), (0, 0), (1, 1), (0, 0)))


def rim_backward(volume):
    grown = extended(volume, (("slab", 0), ("mp", 1)), 1)
    return jnp.pad(grown, ((0, 0), (0, 0), (1, 1), (0, 0)))


def flipped(weight):
    return jnp.transpose(weight[::-1, ::-1, ::-1], (0, 1, 2, 4, 3))


def partition(volume):
    planes, height, breadth, channels = volume.shape
    grid = volume.reshape(planes, height // WIN, WIN, breadth // WIN, WIN, channels).transpose(
        1, 3, 0, 2, 4, 5
    )
    return grid.reshape(height // WIN * (breadth // WIN), planes * WIN * WIN, channels)


def unpartition(windows, shape):
    planes, height, breadth, channels = shape
    grid = windows.reshape(height // WIN, breadth // WIN, planes, WIN, WIN, channels).transpose(
        2, 0, 3, 1, 4, 5
    )
    return grid.reshape(shape)


def region_ids(depth_pos, height_pos, breadth_pos, depth_len, height_len, breadth_len):

    def part_of(places, length):
        return jnp.where(places < length - WIN, 0, jnp.where(places < length - SHIFT, 1, 2))

    return (
        part_of(depth_pos, depth_len)[:, None, None] * 9
        + part_of(height_pos, height_len)[None, :, None] * 3
        + part_of(breadth_pos, breadth_len)[None, None, :]
    ).astype(jnp.int32)


def window_attention(parts, layer, volume, region):
    tag = str(layer)
    window = partition(volume)
    count, length, channels = window.shape
    qkv = matmul(window, parts["qkv_weight" + tag]) + parts["qkv_bias" + tag]
    qkv = qkv.reshape(count, length, 3, HEADS, HDIM)
    queries, key_rows, value_rows = (qkv[:, :, 0], qkv[:, :, 1], qkv[:, :, 2])
    scores = jnp.einsum("nqhd,nkhd->nhqk", queries, key_rows, precision=HIGH) * HDIM ** (-0.5)
    if region is not None:
        labels_win = partition(region[..., None])[..., 0]
        same = labels_win[:, None, :, None] == labels_win[:, None, None, :]
        scores = scores + jnp.where(same, 0.0, -100.0)
    weights = jax.nn.softmax(scores, -1)
    mixed_rows = jnp.einsum("nhqk,nkhd->nqhd", weights, value_rows, precision=HIGH).reshape(
        count, length, channels
    )
    output = matmul(mixed_rows, parts["proj_weight" + tag]) + parts["proj_bias" + tag]
    return unpartition(output, volume.shape)


def pre_norm(parts, layer, tokens):
    tag = str(layer)
    return norm_rows(tokens, parts["first_gain" + tag], parts["first_bias" + tag])


def mlp_block(parts, layer, tokens, attended):
    tag = str(layer)
    middle = tokens + attended
    normed = norm_rows(middle, parts["second_gain" + tag], parts["second_bias" + tag])
    hidden = jax.nn.gelu(
        matmul(normed, parts["hidden_weight" + tag]) + parts["hidden_bias" + tag], approximate=False
    )
    return middle + matmul(hidden, parts["output_weight" + tag]) + parts["output_bias" + tag]


def head_loss(parts, tokens, first_sum, second_sum, voxels, labels, valid):
    average = first_sum / voxels
    spread = second_sum / voxels - average * average
    normed = (tokens - average) * lax.rsqrt(spread + eps_norm) * parts["inorm_gain"] + parts[
        "inorm_bias"
    ]
    logits = (
        matmul(jax.nn.gelu(normed, approximate=False), parts["head_weight"]) + parts["head_bias"]
    )
    logp = jax.nn.log_softmax(logits, -1)
    picked = jnp.sum(
        jnp.where(labels[..., None] == jnp.arange(CLASSES, dtype=jnp.int32), logp, 0.0), -1
    )
    return -picked * valid.astype(logp.dtype)


def roll_ahead(volume):
    lower = passed_along(volume[:SHIFT], "slab", -1)
    volume = jnp.concatenate([volume[SHIFT:], lower], 0)
    upper = passed_along(volume[:, :SHIFT], "mp", -1)
    volume = jnp.concatenate([volume[:, SHIFT:], upper], 1)
    return jnp.roll(volume, -SHIFT, 2)


def roll_behind(volume):
    trailing = passed_along(volume[-SHIFT:], "slab", 1)
    volume = jnp.concatenate([trailing, volume[:-SHIFT]], 0)
    bottom = passed_along(volume[:, -SHIFT:], "mp", 1)
    volume = jnp.concatenate([bottom, volume[:, :-SHIFT]], 1)
    return jnp.roll(volume, SHIFT, 2)


def adamw(param, grad, first, second, scale):
    grad = grad * scale
    first = beta_one * first + (1.0 - beta_one) * grad
    second = beta_two * second + (1.0 - beta_two) * grad * grad
    first_hat = first / (1.0 - beta_one**STEP)
    second_hat = second / (1.0 - beta_two**STEP)
    param = param - learn_rate * (
        first_hat / (jnp.sqrt(second_hat) + adam_eps) + decay_rate * param
    )
    return (param, first, second)


def conv_apply(flat, padded, which):
    parts = carve(flat)
    tag = str(which)
    return conv_valid(padded, parts["conv_weight" + tag]) + parts["conv_bias" + tag]


def on_device(feats, labels, valid, params, moment_one, moment_two):
    parts = carve(params)
    tokens, embed_back = jax.vjp(lambda flat: embed(carve(flat), feats), params)
    planes, height, breadth = tokens.shape[:3]
    depth_pos = lax.axis_index("slab") * planes + jnp.arange(planes, dtype=jnp.int32)
    height_pos = lax.axis_index("mp") * height + jnp.arange(height, dtype=jnp.int32)
    region = region_ids(
        depth_pos,
        height_pos,
        jnp.arange(breadth, dtype=jnp.int32),
        planes * lax.axis_size("slab"),
        height * lax.axis_size("mp"),
        breadth,
    )
    kept = []
    for layer in range(LAYERS):
        shifted = layer % 2 == 1
        normed, pre_back = jax.vjp(
            lambda flat, state, depth_l=layer: pre_norm(carve(flat), depth_l, state), params, tokens
        )
        if shifted:
            normed = roll_ahead(normed)
        attended, attn_back = jax.vjp(
            lambda flat, state, depth_l=layer, marks=region if shifted else None: window_attention(
                carve(flat), depth_l, state, marks
            ),
            params,
            normed,
        )
        if shifted:
            attended = roll_behind(attended)
        tokens, post_back = jax.vjp(
            lambda flat, state, extra, depth_l=layer: mlp_block(carve(flat), depth_l, state, extra),
            params,
            tokens,
            attended,
        )
        kept.append((shifted, pre_back, attn_back, post_back))
    conv_kept = []
    current = tokens
    for which in range(2):
        padded = rim_forward(current)
        result, conv_back = jax.vjp(
            lambda flat, grown=padded, index=which: conv_apply(flat, grown, index), params
        )
        if which == 0:
            current, gelu_back = jax.vjp(
                lambda value: jax.nn.gelu(value, approximate=False), result
            )
        else:
            current = tokens + result
        conv_kept.append(conv_back)
    tokens = current
    local_one = jnp.sum(tokens, (0, 1, 2))
    local_two = jnp.sum(tokens * tokens, (0, 1, 2))
    local_count = jnp.sum(valid).astype(jnp.float32)
    first_sum, second_sum, valid_count = lax.psum(
        (local_one, local_two, local_count), ("slab", "mp")
    )
    voxels = planes * height * breadth * lax.axis_size("slab") * lax.axis_size("mp")
    loss_local, tail_back = jax.vjp(
        lambda flat, state, sum_one, sum_two: jnp.sum(
            head_loss(carve(flat), state, sum_one, sum_two, voxels, labels, valid)
        ),
        params,
        tokens,
        first_sum,
        second_sum,
    )
    gradient, grad_tokens, grad_one, grad_two = tail_back(jnp.float32(1.0) / valid_count)
    loss_sum, grad_one, grad_two = lax.psum((loss_local, grad_one, grad_two), ("slab", "mp"))
    grad_tokens = grad_tokens + grad_one + 2.0 * tokens * grad_two
    grad_inner = grad_tokens
    for which in (1, 0):
        (grad_conv,) = conv_kept[which](grad_inner)
        gradient = gradient + grad_conv
        passed = conv_valid(rim_backward(grad_inner), flipped(parts["conv_weight" + str(which)]))
        if which == 1:
            (grad_inner,) = gelu_back(passed)
        else:
            grad_tokens = grad_tokens + passed
    for shifted, pre_back, attn_back, post_back in reversed(kept):
        grad_post, grad_skip, grad_attended = post_back(grad_tokens)
        if shifted:
            grad_attended = roll_ahead(grad_attended)
        grad_attn, grad_normed = attn_back(grad_attended)
        if shifted:
            grad_normed = roll_behind(grad_normed)
        grad_pre, grad_inner = pre_back(grad_normed)
        gradient = gradient + grad_post + grad_attn + grad_pre
        grad_tokens = grad_skip + grad_inner
    (grad_embed,) = embed_back(grad_tokens)
    gradient = gradient + grad_embed
    gradient = lax.psum(gradient, ("slab", "mp"))
    grad_norm = jnp.sqrt(jnp.sum(gradient * gradient))
    scale = jnp.minimum(1.0, clip_norm / (grad_norm + 1e-06))
    new_params, new_first, new_second = adamw(params, gradient, moment_one, moment_two, scale)
    return (loss_sum, valid_count, grad_norm, new_params, new_first, new_second)


def solution(mesh):
    placed = (
        P("slab", "mp", None, None),
        P("slab", "mp", None),
        P("slab", "mp", None),
        P(),
        P(),
        P(),
    )
    return jax.shard_map(
        on_device,
        mesh=mesh,
        in_specs=placed,
        out_specs=(P(), P(), P(), P(), P(), P()),
        check_vma=False,
    )
```

profile of v0, /device:TPU:0, one launch (start us, length us, event | category | flops | bytes accessed | tf_op | source)
XLA Modules:
  0.0 810.5 jit_solution(18002868185203486566)
XLA Ops:
  7.2 2.4 fusion.471
  22.5 3.5 multiply_reduce_fusion.5
  46.7 6.0 collective-permute-start
  59.4 2.6 reshape.990
  69.0 4.7 fusion.2
  74.5 2.3 fusion.6
  79.4 2.5 reverse_bitcast_fusion.1
  81.8 2.6 reshape.989
  93.8 2.5 reverse_bitcast_fusion
  127.9 3.5 multiply_reduce_fusion.4
  147.8 3.8 collective-permute-done.5
  154.8 2.6 collective-permute-done.7
  173.1 3.5 collective-permute-start.8
  178.5 3.8 collective-permute-done.9
  182.3 3.1 collective-permute-start.10
  204.5 44.3 %all-reduce.115 = (f32[96]{0:T(128)S(1)}, f32[96]{0:T(128)S(1)}, f32[]{:T(128)}) all-reduce(f32[96]{0:T(128)S(1)} %get-tuple-element.42, f32[96]{0:T(128)S(1)} %get-tuple-element.41, f32[]{:T(128)S(6)} %convert_element_type.12), channel_id=1, replica_groups=mesh['slab'=8,'mp'=4] {'slab','mp'}, use_global_device_ids=true, to_apply=%region_23.24 | all-reduce | flops 193 | bytes 1544 | tf_op jit(solution)/shard_map/psum | solution.py:313
  255.5 3.2 multiply_reduce_fusion.21
  261.9 38.7 %all-reduce.114 = (f32[]{:T(128)}, f32[96]{0:T(128)S(1)}, f32[96]{0:T(128)S(1)}) all-reduce(f32[]{:T(128)} %multiply_reduce_fusion.30, f32[96]{0:T(128)S(1)} %broadcast_multiply_fusion.8, f32[96]{0:T(128)S(1)} %get-tuple-element.72), channel_id=1, replica_groups=mesh['slab'=8,'mp'=4] {'slab','mp'}, use_global_device_ids=true, to_apply=%region_28.29 | all-reduce | flops 193 | bytes 1544 | tf_op jit(solution)/shard_map/psum | solution.py:327
  314.6 4.2 collective-permute-start.12
  332.8 3.4 reshape.993
  356.7 2.3 fusion.488
  368.6 4.5 collective-permute-start.16
  380.2 4.8 collective-permute-start.18
  387.6 3.4 reshape.994
  420.7 5.2 convolution_bitcast_fusion.17
  426.0 4.0 multiply_reduce_fusion.3
  430.8 3.4 convolution_bitcast_fusion.16
  437.7 4.9 copy.163
  442.7 4.0 dot_general.909
  446.7 2.7 fusion.447
  453.7 3.2 convolution_bitcast_fusion.2
  462.7 4.0 collective-permute-start.20
  478.9 2.9 collective-permute-start.21
  486.4 5.5 fusion.80
  492.0 4.1 multiply_reduce_fusion.2
  496.1 3.9 convolution_bitcast_fusion.14
  500.1 3.5 convolution_bitcast_fusion.13
  510.1 2.5 fusion.492
  539.3 3.1 convolution_bitcast_fusion.1
  550.3 3.9 convolution_bitcast_fusion.12
  554.2 4.1 multiply_reduce_fusion.1
  559.3 3.0 convolution_bitcast_fusion.11
  565.9 4.1 copy.178
  570.1 3.4 dot_general.944
  586.1 64.1 %add_add_fusion = f32[872558]{0:T(1024)} fusion(f32[384]{0:T(512)} %get-tuple-element.7, f32[384]{0:T(512)} %get-tuple-element.6, f32[36864]{0:T(1024)S(1)} %reshape.1016, f32[96]{0:T(128)} %get-tuple-element.24, f32[96]{0:T(128)} %get-tuple-element.40, f32[27648]{0:T(1024)S(1)} %reshape.1015, f32[288]{0:T(512)S(1)} %reduce_sum.810, f32[9216]{0:T(1024)S(1)} %reshape.1012, ...), kind=kLoop, calls=%fused_computation.6 | loop fusion | flops 40137680 | bytes 6980464 | tf_op jit(solution)/shard_map/add | solution.py:349
  650.2 139.0 %all-reduce.118.cloned.1.call-done = f32[872558]{0:T(1024)} async-done(((f32[872558]{0:T(1024)}), f32[872558]{0:T(1024)}) %all-reduce.118.cloned.1.call-update) | async-done | bytes 3490248 | tf_op jit(solution)/shard_map/psum | solution.py:350
  789.3 3.5 multiply_reduce_fusion
  793.5 8.7 %multiply_subtract_fusion = (f32[872558]{0:T(1024)}, f32[872558]{0:T(1024)}, f32[872558]{0:T(1024)}) fusion(f32[872558]{0:T(1024)} %param.9, f32[872558]{0:T(1024)} %all-reduce.118.cloned.1.call-done, f32[]{:T(128)S(6)} %min.3, f32[872558]{0:T(1024)} %param.10, f32[872558]{0:T(1024)} %param.11), kind=kLoop, calls=%fused_computation.3 | loop fusion | flops 13960928 | bytes 24431628 | tf_op jit(solution)/shard_map/sub | solution.py:245
  (863 shorter events, 339.2 us)
Async XLA Ops:
  7.2 782.1 %all-reduce.118.cloned.1.call-start = ((), (), s32[]{:S(2)}) async-start(), calls=%async_computation | async-start | bytes 6987776 | tf_op jit(solution)/shard_map/psum | solution.py:350
  44.6 74.1 %copy-start.18 = (f32[7,7,7,96]{3,2,1,0:T(8,128)}, f32[7,7,7,96]{3,2,1,0:T(8,128)S(1)}, u32[]{:S(2)}) copy-start(f32[7,7,7,96]{3,2,1,0:T(8,128)S(1)} %get-tuple-element.159) | copy-start | bytes 395140
  46.7 15.3 %collective-permute-start = (f32[3,7,7,96]{3,2,1,0:T(8,128)}, f32[3,7,7,96]{3,2,1,0:T(8,128)}, u32[]{:S(2)}, u32[]{:S(2)}) collective-permute-start(f32[3,7,7,96]{3,2,1,0:T(8,128)} %slice.1342), channel_id=1, source_target_pairs={{0,28},{4,0},{8,4},{12,8},{16,12},{20,16},{24,20},{28,24},{1,29},{... | collective-permute-start | bytes 169352 | tf_op jit(solution)/shard_map/ppermute | solution.py:50
  62.8 2.8 collective-permute-start.1
  79.4 9.8 %collective-permute-start.2 = (f32[3,7,7,96]{3,2,1,0:T(8,128)}, f32[3,7,7,96]{3,2,1,0:T(8,128)}, u32[]{:S(2)}, u32[]{:S(2)}) collective-permute-start(f32[3,7,7,96]{3,2,1,0:T(8,128)} %slice.1060), channel_id=1, source_target_pairs={{0,4},{4,8},{8,12},{12,16},{16,20},{20,24},{24,28},{28,0},{1,5},{5... | collective-permute-start | bytes 169352 | tf_op jit(solution)/shard_map/ppermute | solution.py:50
  81.8 23.3 %copy-start.125 = (f32[9216]{0:T(1024)S(1)}, f32[9216]{0:T(1024)}, u32[]{:S(2)}) copy-start(f32[9216]{0:T(1024)} %get-tuple-element.116) | copy-start | bytes 110596
  81.8 24.0 %copy-start.123 = (f32[9216]{0:T(1024)S(1)}, f32[9216]{0:T(1024)}, u32[]{:S(2)}) copy-start(f32[9216]{0:T(1024)} %copy-done.122) | copy-start | bytes 110596
  81.8 24.7 %copy-start.71 = (f32[27648]{0:T(1024)S(1)}, f32[27648]{0:T(1024)}, u32[]{:S(2)}) copy-start(f32[27648]{0:T(1024)} %copy-done.70) | copy-start | bytes 331780
  92.3 25.5 %collective-permute-start.3 = (f32[7,3,7,96]{3,2,1,0:T(8,128)}, f32[7,3,7,96]{3,2,1,0:T(8,128)}, u32[]{:S(2)}, u32[]{:S(2)}) collective-permute-start(f32[7,3,7,96]{3,2,1,0:T(8,128)} %slice.1352), channel_id=1, source_target_pairs={{0,1},{1,2},{2,3},{3,0},{4,5},{5,6},{6,7},{7,4},{8,9},{9,10},{10,1... | collective-permute-start | bytes 169352 | tf_op jit(solution)/shard_map/ppermute | solution.py:50
  106.5 16.0 %copy-start.206 = (f32[96]{0:T(128)S(1)}, f32[96]{0:T(128)}, u32[]{:S(2)}) copy-start(f32[96]{0:T(128)} %get-tuple-element.92) | copy-start | bytes 1156
  108.2 15.4 %copy-start.110 = (f32[96,384,1,1]{1,0,2,3:T(8,128)}, f32[96,384,1,1]{1,0,2,3:T(8,128)S(1)}, u32[]{:S(2)}) copy-start(f32[96,384,1,1]{1,0,2,3:T(8,128)S(1)} %reshape.1020) | copy-start | bytes 442372
  137.9 16.4 %copy-start.17 = (f32[3,3,3,96,96]{4,3,2,1,0:T(8,128)S(1)}, f32[3,3,3,96,96]{4,3,2,1,0:T(8,128)}, u32[]{:S(2)}) copy-start(f32[3,3,3,96,96]{4,3,2,1,0:T(8,128)} %reshape.989) | copy-start | bytes 2985988
  139.1 15.7 %copy-start.30 = (f32[7,7,7,96]{3,2,1,0:T(8,128)}, f32[7,7,7,96]{3,2,1,0:T(8,128)S(1)}, u32[]{:S(2)}) copy-start(f32[7,7,7,96]{3,2,1,0:T(8,128)S(1)} %get-tuple-element.77) | copy-start | bytes 395140
  139.1 18.5 %copy-start.92 = (f32[7,7,7]{2,1,0:T(8,128)}, f32[7,7,7]{2,1,0:T(8,128)S(1)}, u32[]{:S(2)}) copy-start(f32[7,7,7]{2,1,0:T(8,128)S(1)} %broadcast_multiply_fusion) | copy-start | bytes 4120
  139.4 18.2 %copy-start.144 = (f32[7,7,7]{2,1,0:T(8,128)}, f32[7,7,7]{2,1,0:T(8,128)S(1)}, u32[]{:S(2)}) copy-start(f32[7,7,7]{2,1,0:T(8,128)S(1)} %multiply_reduce_fusion.23) | copy-start | bytes 4120
  139.4 18.2 %copy-start.142 = (f32[7,7,7]{2,1,0:T(8,128)}, f32[7,7,7]{2,1,0:T(8,128)S(1)}, u32[]{:S(2)}) copy-start(f32[7,7,7]{2,1,0:T(8,128)S(1)} %fusion.395) | copy-start | bytes 4120
  142.8 18.1 %copy-start.56 = (f32[7,7,7,384]{3,2,1,0:T(8,128)}, f32[7,7,7,384]{3,2,1,0:T(8,128)S(1)}, u32[]{:S(2)}) copy-start(f32[7,7,7,384]{3,2,1,0:T(8,128)S(1)} %fusion.86) | copy-start | bytes 1580548
  144.4 3.4 collective-permute-start.4
  145.9 5.8 collective-permute-start.5
  151.7 3.1 collective-permute-start.6
  153.0 4.5 collective-permute-start.7
  168.9 17.9 %copy-start.16 = (f32[3,3,3,96,96]{4,3,2,1,0:T(8,128)S(1)}, f32[3,3,3,96,96]{4,3,2,1,0:T(8,128)}, u32[]{:S(2)}) copy-start(f32[3,3,3,96,96]{4,3,2,1,0:T(8,128)} %reshape.990) | copy-start | bytes 2985988
  172.1 15.3 %copy-start.79 = (f32[7,7,7,96]{3,2,1,0:T(8,128)}, f32[7,7,7,96]{3,2,1,0:T(8,128)S(1)}, u32[]{:S(2)}) copy-start(f32[7,7,7,96]{3,2,1,0:T(8,128)S(1)} %get-tuple-element.169) | copy-start | bytes 395140
  173.1 30.0 %copy-start.5 = (f32[7,7,7,96]{3,2,1,0:T(8,128)}, f32[7,7,7,96]{3,2,1,0:T(8,128)S(1)}, u32[]{:S(2)}) copy-start(f32[7,7,7,96]{3,2,1,0:T(8,128)S(1)} %multiply_multiply_fusion.39) | copy-start | bytes 395140
  173.1 5.4 collective-permute-start.8
  176.6 5.8 collective-permute-start.9
  182.3 5.0 collective-permute-start.10
  185.5 4.0 collective-permute-start.11
  200.8 48.5 %copy-start.193 = (f32[96]{0:T(128)S(1)}, f32[96]{0:T(128)}, u32[]{:S(2)}) copy-start(f32[96]{0:T(128)} %get-tuple-element.82) | copy-start | bytes 1156
  200.8 48.5 %copy-start.194 = (f32[96]{0:T(128)S(1)}, f32[96]{0:T(128)}, u32[]{:S(2)}) copy-start(f32[96]{0:T(128)} %get-tuple-element.83) | copy-start | bytes 1156
  200.8 50.6 %copy-start.212 = (f32[14]{0:T(128)S(1)}, f32[14]{0:T(128)}, u32[]{:S(2)}) copy-start(f32[14]{0:T(128)} %slice.1209) | copy-start | bytes 172
  201.4 53.0 %copy-start.126 = (s32[7,7,7]{2,1,0:T(8,128)S(1)}, s32[7,7,7]{2,1,0:T(8,128)}, u32[]{:S(2)}) copy-start(s32[7,7,7]{2,1,0:T(8,128)} %param.8) | copy-start | bytes 4120
  302.3 25.0 %copy-start.2 = (f32[7,7,7,96]{3,2,1,0:T(8,128)}, f32[7,7,7,96]{3,2,1,0:T(8,128)S(1)}, u32[]{:S(2)}) copy-start(f32[7,7,7,96]{3,2,1,0:T(8,128)S(1)} %get-tuple-element.53) | copy-start | bytes 395140
  314.6 12.7 %collective-permute-start.12 = (f32[1,7,7,96]{3,2,1,0:T(8,128)S(1)}, f32[1,7,7,96]{3,2,1,0:T(8,128)S(1)}, u32[]{:S(2)}, u32[]{:S(2)}) collective-permute-start(f32[1,7,7,96]{3,2,1,0:T(8,128)S(1)} %get-tuple-element.144), channel_id=1, source_target_pairs={{0,4},{4,8},{8,12},{12,16},{16,20},{20,24},{24,28},{1,5},{5,9},{9,... | collective-permute-start | bytes 56456 | tf_op jit(solution)/shard_map/ppermute | solution.py:38
  318.8 8.5 %collective-permute-start.13 = (f32[1,7,7,96]{3,2,1,0:T(8,128)S(1)}, f32[1,7,7,96]{3,2,1,0:T(8,128)S(1)}, u32[]{:S(2)}, u32[]{:S(2)}) collective-permute-start(f32[1,7,7,96]{3,2,1,0:T(8,128)S(1)} %get-tuple-element.145), channel_id=1, source_target_pairs={{4,0},{8,4},{12,8},{16,12},{20,16},{24,20},{28,24},{5,1},{9,5},{13... | collective-permute-start | bytes 56456 | tf_op jit(solution)/shard_map/ppermute | solution.py:40
  327.9 8.4 %collective-permute-start.14 = (f32[9,1,7,96]{3,2,1,0:T(8,128)}, f32[9,1,7,96]{3,2,1,0:T(8,128)S(1)}, u32[]{:S(2)}, u32[]{:S(2)}) collective-permute-start(f32[9,1,7,96]{3,2,1,0:T(8,128)} %get-tuple-element.135), channel_id=1, source_target_pairs={{0,1},{1,2},{2,3},{4,5},{5,6},{6,7},{8,9},{9,10},{10,11},{12,13},{... | collective-permute-start | bytes 72584 | tf_op jit(solution)/shard_map/ppermute | solution.py:38
  329.2 7.1 collective-permute-start.15
  359.0 27.3 %copy-start.13 = (f32[7,7,7,96]{3,2,1,0:T(8,128)}, f32[7,7,7,96]{3,2,1,0:T(8,128)S(1)}, u32[]{:S(2)}) copy-start(f32[7,7,7,96]{3,2,1,0:T(8,128)S(1)} %get-tuple-element.192) | copy-start | bytes 395140
  368.6 11.0 %collective-permute-start.16 = (f32[1,7,7,96]{3,2,1,0:T(8,128)S(1)}, f32[1,7,7,96]{3,2,1,0:T(8,128)S(1)}, u32[]{:S(2)}, u32[]{:S(2)}) collective-permute-start(f32[1,7,7,96]{3,2,1,0:T(8,128)S(1)} %get-tuple-element.142), channel_id=1, source_target_pairs={{0,4},{4,8},{8,12},{12,16},{16,20},{20,24},{24,28},{1,5},{5,9},{9,... | collective-permute-start | bytes 56456 | tf_op jit(solution)/shard_map/ppermute | solution.py:38
  373.1 6.4 collective-permute-start.17
  380.2 10.9 %collective-permute-start.18 = (f32[9,1,7,96]{3,2,1,0:T(8,128)}, f32[9,1,7,96]{3,2,1,0:T(8,128)S(1)}, u32[]{:S(2)}, u32[]{:S(2)}) collective-permute-start(f32[9,1,7,96]{3,2,1,0:T(8,128)} %get-tuple-element.133), channel_id=1, source_target_pairs={{0,1},{1,2},{2,3},{4,5},{5,6},{6,7},{8,9},{9,10},{10,11},{12,13},{... | collective-permute-start | bytes 72584 | tf_op jit(solution)/shard_map/ppermute | solution.py:38
  385.0 6.1 collective-permute-start.19
  462.1 16.1 %copy-start.169 = (f32[3,6,16]{2,1,0:T(8,128)S(1)}, f32[3,6,16]{2,1,0:T(8,128)}, u32[]{:S(2)}) copy-start(f32[3,6,16]{2,1,0:T(8,128)} %get-tuple-element.127) | copy-start | bytes 3460
  462.7 16.1 %collective-permute-start.20 = (f32[3,7,7,96]{3,2,1,0:T(8,128)}, f32[3,7,7,96]{3,2,1,0:T(8,128)S(1)}, u32[]{:S(2)}, u32[]{:S(2)}) collective-permute-start(f32[3,7,7,96]{3,2,1,0:T(8,128)} %slice.1548), channel_id=1, source_target_pairs={{0,28},{4,0},{8,4},{12,8},{16,12},{20,16},{24,20},{28,24},{1,29},{... | collective-permute-start | bytes 169352 | tf_op jit(solution)/shard_map/ppermute | solution.py:50
  478.9 5.0 collective-permute-start.21
  503.6 30.4 %copy-start.19 = (f32[7,7,7,96]{3,2,1,0:T(8,128)S(1)}, f32[7,7,7,96]{3,2,1,0:T(8,128)}, u32[]{:S(2)}) copy-start(f32[7,7,7,96]{3,2,1,0:T(8,128)} %copy-done.18) | copy-start | bytes 395140
  510.1 7.5 collective-permute-start.22
  520.8 10.3 %collective-permute-start.23 = (f32[7,3,7,96]{3,2,1,0:T(8,128)}, f32[7,3,7,96]{3,2,1,0:T(8,128)}, u32[]{:S(2)}, u32[]{:S(2)}) collective-permute-start(f32[7,3,7,96]{3,2,1,0:T(8,128)} %slice.1555), channel_id=1, source_target_pairs={{0,1},{1,2},{2,3},{3,0},{4,5},{5,6},{6,7},{7,4},{8,9},{9,10},{10,1... | collective-permute-start | bytes 169352 | tf_op jit(solution)/shard_map/ppermute | solution.py:50
  (190 other events, 1087.9 us)
Sparse Core Ops, SparseCore 0:
  650.3 138.8 all-reduce.117
where the time goes:
time: 824 us; the launch traced here: 811 us
  matrix products  232 us (28%)
  waiting for transfers between devices  155 us (19%)
  other arithmetic  137 us (17%)
  local copies, waits for them, and re-layouts  130 us (16%)
  blocking collectives  83 us (10%)
  starting transfers between devices  51.6 us (6%)
  between operations  21.9 us (3%)
    dot_general x204, matrix products, matmul(): return jnp.einsum('...c,cd->...d', tokens, weight, precision=HIGH)  169 us
    psum x1, waiting for transfers between devices, on_device(): gradient = lax.psum(gradient, ('slab', 'mp'))  139 us
    add x1, other arithmetic, on_device(): gradient = gradient + grad_embed  64.1 us
    reshape x34, local copies, waits for them, and re-layouts, carve(): parts[name] = flat[offset:offset + count].reshape(shape)  47.2 us
    psum x1, blocking collectives, on_device(): lax.psum((local_one, local_two, local_count), ('slab', 'mp'))  44.3 us
    psum x1, blocking collectives, on_device(): lax.psum((loss_local, grad_one, grad_two), ('slab', 'mp'))  38.7 us
    dot_general x9, matrix products, window_attention(): jnp.einsum('nhqk,nkhd->nqhd', weights, value_rows, precision=HIGH)  33.6 us
    dot_general x9, matrix products, window_attention(): jnp.einsum('nqhd,nkhd->nhqk', queries, key_rows, precision=HIGH)  29.8 us
  transfers between devices with their start and end apart: 25, of which 8 were waited for; matrix products, arithmetic and copies ran while one was open for 12% of the time, Pallas kernels for 0%

commit v1 on v0

v1 whole, which is shorter than its diff:
```python
import functools

import jax
import jax.numpy as jnp
from jax import lax
from jax.experimental import pallas as pl
from jax.experimental.pallas import tpu as pltpu
from jax.sharding import PartitionSpec as P

EMB = 96
HEADS = 6
HDIM = 16
HID = 384
MERGE = 384
CLASSES = 14
WIN = 7
SHIFT = 3
LAYERS = 3
STEP = 10

F32 = jnp.float32
BF16 = jnp.bfloat16
eps_norm = 1e-05
beta_one = 0.9
beta_two = 0.999
adam_eps = 1e-08
learn_rate = 0.05
decay_rate = 0.05
clip_norm = 0.01

VOX = WIN * WIN * WIN
ROWS = 384
BLK = 128
WIDE = 128
PLANE = WIN * WIN
FAR = WIN - SHIFT
ROWS_A = SHIFT * FAR * WIN
ROWS_B = FAR * SHIFT * WIN
ROWS_C = SHIFT * SHIFT * WIN

MERGE_ROWS = 392
LAYER_ROWS = 1165
TAP_ROWS = 27 * EMB
GROUPS = 2280
NPARAM = 872558
FLAT_ROWS = GROUPS * 3
LAYER_BASE = (98, 389, 680)
CONV_BASE = (971, 1620)
CUTS = (0, 392, 688, 976, 2280)

R_QKV, R_QKVB, R_PROJ, R_PROJB = 4, 292, 295, 391
R_HID, R_HIDB, R_OUT, R_OUTB = 392, 776, 780, 1164

VMEM = 56 * 1024 * 1024


def iota(shape, dim):
    return lax.broadcasted_iota(jnp.int32, shape, dim)


def split(x):
    hi = x.astype(BF16)
    return hi, (x - hi.astype(F32)).astype(BF16)


def pair(x):
    return jnp.concatenate(split(x), 1)


def fold(y):
    half = y.shape[1] // 2
    return y[:, :half] + y[:, half:]


def fold_rows(y):
    half = y.shape[0] // 2
    return y[:half] + y[half:]


def dot(a, b):
    return jnp.dot(a, b, preferred_element_type=F32)


def dot_nt(a, b):
    return lax.dot_general(a, b, (((1,), (1,)), ((), ())), preferred_element_type=F32)


def weight_nn(w):
    top = pair(w)
    return jnp.concatenate([top, top], 0)


def weight_nt(w):
    hi, lo = split(w)
    return jnp.concatenate(
        [jnp.concatenate([hi, hi], 1), jnp.concatenate([lo, lo], 1)], 0
    )


def mm(x, w):
    return fold(dot(pair(x), weight_nn(w)))


def mm_nt(x, w):
    return fold(dot_nt(pair(x), weight_nt(w)))


def rows_t(x):
    return jnp.concatenate(split(x.T), 0)


def mm_tn(xt, y):
    return fold_rows(fold(dot(xt, pair(y))))


def deep(w):
    return jnp.concatenate([w, jnp.zeros((WIDE - EMB, w.shape[1]), F32)], 0)


def roll(x, shift, axis):
    return pltpu.roll(x, shift, axis)


def four_to_three(y):
    lane = iota(y[0].shape, 1)
    a = jnp.where(lane < 96, y[0], roll(y[1], 96, 1))
    b = jnp.where(lane < 64, roll(y[1], 96, 1), roll(y[2], 64, 1))
    c = jnp.where(lane < 32, roll(y[2], 64, 1), roll(y[3], 32, 1))
    return a, b, c


def three_to_four(x):
    lane = iota(x[0].shape, 1)
    live = lane < EMB
    a = x[0]
    b = jnp.where(lane < 32, roll(x[0], 32, 1), roll(x[1], 32, 1))
    c = jnp.where(lane < 64, roll(x[1], 64, 1), roll(x[2], 64, 1))
    d = roll(x[2], 96, 1)
    return tuple(jnp.where(live, v, 0.0) for v in (a, b, c, d))


def hidden_rows(ref, start, count):
    return jnp.concatenate(
        four_to_three([ref[pl.ds(start + c, count, stride=4), :] for c in range(4)]), 1
    )


def put_hidden_rows(ref, start, count, x):
    parts = three_to_four([x[:, i * WIDE : (i + 1) * WIDE] for i in range(3)])
    for c in range(4):
        ref[pl.ds(start + c, count, stride=4), :] = parts[c]


def flatten(ref, start, groups, out):
    parts = four_to_three([ref[pl.ds(start + c, groups, stride=4), :] for c in range(4)])
    for c in range(3):
        out[pl.ds(c, groups, stride=3), :] = parts[c]


def norm_stats(x):
    live = iota(x.shape, 1) < EMB
    mean = jnp.sum(x, 1, keepdims=True) * (1.0 / EMB)
    centred = jnp.where(live, x - mean, 0.0)
    var = jnp.sum(centred * centred, 1, keepdims=True) * (1.0 / EMB)
    inv = lax.rsqrt(var + eps_norm)
    return centred * inv, inv


def norm(x, gain, bias):
    hat, _ = norm_stats(x)
    return hat * gain + bias


def norm_back(hat, inv, gain, grad):
    up = grad * gain
    one = jnp.sum(up, 1, keepdims=True) * (1.0 / EMB)
    two = jnp.sum(up * hat, 1, keepdims=True) * (1.0 / EMB)
    live = iota(hat.shape, 1) < EMB
    return jnp.where(live, inv * (up - one - hat * two), 0.0)


def colsum(x):
    return jnp.sum(x, 0, keepdims=True)


def gelu(x):
    return 0.5 * x * (1.0 + lax.erf(x * (0.5**0.5)))


def gelu_both(x):
    cdf = 0.5 * (1.0 + lax.erf(x * (0.5**0.5)))
    slope = cdf + x * (jnp.exp(x * x * -0.5) * 0.3989422804014327)
    return x * cdf, slope


def head_groups(x):
    lane = iota(x.shape, 1)
    swapped = roll(x, 64, 1)
    return jnp.where(lane < 64, x, swapped), jnp.where(lane < 64, swapped, x)


def as_left(x):
    both = []
    low = iota(x.shape, 1) < 64
    for part in head_groups(x):
        hi = part.astype(BF16).astype(F32)
        one = jnp.where(low, hi, part - hi).astype(BF16)
        both.append(jnp.concatenate([one, one], 1))
    return both


def as_right(x):
    return [pair(part) for part in head_groups(x)]


def head_mask(h, width):
    lane = iota((1, width), 1)
    lane = jnp.bitwise_and(lane, 63)
    low = jnp.bitwise_and(h, 3) * HDIM
    return jnp.where((lane >= low) & (lane < low + HDIM), 1.0, 0.0)


def own_lanes(h):
    lane = iota((1, WIDE), 1)
    return jnp.where((lane >= h * HDIM) & (lane < (h + 1) * HDIM), 1.0, 0.0)


def scores(q, k, h, rows, region):
    left = q * head_mask(h, 2 * WIDE).astype(BF16)
    s = dot_nt(left, k)
    if region is not None:
        region_rows, region_lanes = region
        here = region_rows[rows, 0:1]
        s = s + jnp.where(here == region_lanes[0:1, :], 0.0, -100.0)
    return jnp.where(iota(s.shape, 1) < VOX, s, -1e30)


def attention(normed, layer, save, lse, mixed, left, right, values, region=None):
    x = pair(normed)
    qkv = []
    for i in range(3):
        w = deep(layer[pl.ds(R_QKV + i, EMB, stride=3), :])
        y = fold(dot(x, weight_nn(w))) + layer[R_QKVB + i : R_QKVB + i + 1, :]
        if i == 0:
            y = y * HDIM**-0.5
        save[:, i * WIDE : (i + 1) * WIDE] = y
        qkv.append(y)
    for g, part in enumerate(as_left(qkv[0])):
        left[g] = part
    for g, part in enumerate(as_right(qkv[1])):
        right[g] = part
    v = pair(qkv[2])
    values[0:ROWS, :] = v
    values[ROWS : 2 * ROWS, :] = v
    mixed[...] = jnp.zeros_like(mixed)
    lse[...] = jnp.zeros_like(lse)

    def per_head(h, carry):
        g = lax.div(h, 4)
        lanes = own_lanes(h)
        at_h = jnp.where(iota((1, WIDE), 1) == h, 1.0, 0.0)
        for b in range(ROWS // BLK):
            rows = slice(b * BLK, (b + 1) * BLK)
            s = scores(left[g, rows, :], right[g], h, rows, region)
            top = jnp.max(s, 1, keepdims=True)
            e = jnp.exp(s - top)
            total = jnp.sum(e, 1, keepdims=True)
            o = fold(dot(pair(e), values[...]))
            mixed[rows, :] += o * (lanes / total)
            lse[rows, :] += (top + jnp.log(total)) * at_h
        return carry

    lax.fori_loop(0, HEADS, per_head, 0)
    proj = deep(layer[R_PROJ : R_PROJ + EMB, :])
    return mm(mixed[...], proj) + layer[R_PROJB : R_PROJB + 1, :]


def attention_back(grad, normed, layer, save, lse, mixed, sc, grads, at, region=None):
    left, right, gleft, vright, keys, dq, dkv_t, weights, slopes, q_t, do_t, dmix = sc
    proj = deep(layer[R_PROJ : R_PROJ + EMB, :])
    grads[at + R_PROJ : at + R_PROJ + EMB, :] = mm_tn(rows_t(mixed[...]), grad)[:EMB]
    grads[at + R_PROJB : at + R_PROJB + 1, :] = colsum(grad)
    d_mixed = mm_nt(grad, proj)
    dmix[...] = d_mixed
    q, k, v = (save[:, i * WIDE : (i + 1) * WIDE] for i in range(3))
    for g, part in enumerate(as_left(q)):
        left[g] = part
    for g, part in enumerate(as_right(k)):
        right[g] = part
    for g, part in enumerate(as_left(d_mixed)):
        gleft[g] = part
    for g, part in enumerate(as_right(v)):
        vright[g] = part
    kk = pair(k)
    keys[0:ROWS, :] = kk
    keys[ROWS : 2 * ROWS, :] = kk
    for ref, x in ((q_t, q), (do_t, d_mixed)):
        hi, lo = split(x.T)
        ref[0] = hi
        ref[1] = lo
    dq[...] = jnp.zeros_like(dq)
    dkv_t[...] = jnp.zeros_like(dkv_t)

    def per_head(h, carry):
        g = lax.div(h, 4)
        lanes = own_lanes(h)
        at_h = jnp.where(iota((1, WIDE), 1) == h, 1.0, 0.0)
        mask = head_mask(h, 2 * WIDE).astype(BF16)
        for b in range(ROWS // BLK):
            rows = slice(b * BLK, (b + 1) * BLK)
            s = scores(left[g, rows, :], right[g], h, rows, region)
            level = jnp.sum(lse[rows, :] * at_h, 1, keepdims=True)
            p = jnp.exp(s - level)
            dp = dot_nt(gleft[g, rows, :] * mask, vright[g])
            delta = jnp.sum(dmix[rows, :] * mixed[rows, :] * lanes, 1, keepdims=True)
            ds = p * (dp - delta)
            both = pair(ds)
            weights[rows, :] = pair(p)
            slopes[rows, :] = both
            dq[rows, :] += fold(dot(both, keys[...])) * lanes
        here = pl.multiple_of(h * HDIM, HDIM)
        for i, (t, m) in enumerate(((q_t, slopes), (do_t, weights))):
            lhs = jnp.concatenate([t[0, pl.ds(here, HDIM), :], t[1, pl.ds(here, HDIM), :]], 0)
            out = fold_rows(fold(dot(lhs, m[...])))
            dkv_t[i, pl.ds(here, HDIM), :] = out
        return carry

    lax.fori_loop(0, HEADS, per_head, 0)
    d_q = dq[...] * HDIM**-0.5
    d_k = dkv_t[0].T
    d_v = dkv_t[1].T
    x_t = rows_t(normed)
    d_normed = None
    for i, d in enumerate((d_q, d_k, d_v)):
        grads[pl.ds(at + R_QKV + i, EMB, stride=3), :] = mm_tn(x_t, d)[:EMB]
        grads[at + R_QKVB + i : at + R_QKVB + i + 1, :] = colsum(d)
        part = mm_nt(d, deep(layer[pl.ds(R_QKV + i, EMB, stride=3), :]))
        d_normed = part if d_normed is None else d_normed + part
    return d_normed


def mlp(middle, layer, hpre):
    normed = norm(middle, layer[2:3, :], layer[3:4, :])
    w = deep(hidden_rows(layer, R_HID, EMB))
    pre = mm(normed, w) + hidden_rows(layer, R_HIDB, 1)
    hpre[...] = pre
    out = mm(gelu(pre), layer[R_OUT : R_OUT + HID, :])
    return middle + out + layer[R_OUTB : R_OUTB + 1, :]


def mlp_back(grad, middle, hpre, layer, grads, at):
    hat, inv = norm_stats(middle)
    normed = hat * layer[2:3, :] + layer[3:4, :]
    act, slope = gelu_both(hpre[...])
    grads[at + R_OUTB : at + R_OUTB + 1, :] = colsum(grad)
    grads[at + R_OUT : at + R_OUT + HID, :] = mm_tn(rows_t(grad), act).T
    d_pre = mm_nt(grad, layer[R_OUT : R_OUT + HID, :]) * slope
    put_hidden_rows(grads, at + R_HIDB, 1, colsum(d_pre))
    put_hidden_rows(grads, at + R_HID, EMB, mm_tn(rows_t(normed), d_pre)[:EMB])
    d_normed = mm_nt(d_pre, deep(hidden_rows(layer, R_HID, EMB)))
    grads[at + 2 : at + 3, :] = colsum(d_normed * hat)
    grads[at + 3 : at + 4, :] = colsum(d_normed)
    return grad + norm_back(hat, inv, layer[2:3, :], d_normed)


def pre_norm_back(grad, tokens, layer, grads, at):
    hat, inv = norm_stats(tokens)
    grads[at : at + 1, :] = colsum(grad * hat)
    grads[at + 1 : at + 2, :] = colsum(grad)
    return norm_back(hat, inv, layer[0:1, :], grad)


def send_parts(ref, a, b, c):
    far = FAR * WIN
    near = SHIFT * WIN
    for d in range(SHIFT):
        base = d * PLANE
        c[d * near : (d + 1) * near, :] = ref[base : base + near, :]
        a[d * far : (d + 1) * far, :] = ref[base + near : base + PLANE, :]
    for d in range(FAR):
        base = (d + SHIFT) * PLANE
        b[d * near : (d + 1) * near, :] = ref[base : base + near, :]


def take_parts(own, a, b, c, out):
    far = FAR * WIN
    near = SHIFT * WIN
    for d in range(WIN):
        base = d * PLANE
        if d < SHIFT:
            out[base : base + near, :] = c[d * near : (d + 1) * near, :]
            out[base + near : base + PLANE, :] = a[d * far : (d + 1) * far, :]
        else:
            e = d - SHIFT
            out[base : base + near, :] = b[e * near : (e + 1) * near, :]
            out[base + near : base + PLANE, :] = own[base + near : base + PLANE, :]
    out[VOX:, :] = jnp.zeros((ROWS - VOX, WIDE), F32)


def prep_kernel(flat, merge, lay0, lay1, lay2, conv0, conv1):
    spans = [(0, 98)] + [(g, g + 292) for g in LAYER_BASE]
    spans += [(CONV_BASE[0], CONV_BASE[0] + 649), (CONV_BASE[1], GROUPS)]
    for out, (low, high) in zip((merge, lay0, lay1, lay2, conv0, conv1), spans):
        count = high - low
        parts = three_to_four(
            [flat[pl.ds(3 * low + c, count, stride=3), :] for c in range(3)]
        )
        for c in range(4):
            out[pl.ds(c, count, stride=4), :] = parts[c]


def offset(ref, at):
    return ref.at[pl.ds(at, ref.shape[0] - at), :]


class Rows:
    def __init__(self, ref, at):
        self.ref, self.at = ref, at

    def __getitem__(self, key):
        rows, lanes = key
        if isinstance(rows, slice):
            rows = slice(rows.start + self.at, rows.stop + self.at)
        else:
            rows = pl.ds(rows.start + self.at, rows.size, stride=rows.stride)
        return self.ref[rows, lanes]


def merged_norm(x):
    mean = jnp.sum(x, 1, keepdims=True) * (1.0 / MERGE)
    centred = x - mean
    var = jnp.sum(centred * centred, 1, keepdims=True) * (1.0 / MERGE)
    return centred * lax.rsqrt(var + eps_norm)


def first_kernel(
    feats, merge, lay0, lay1,
    dense, tok0, save, lse, mixed, middle, hpre, tok1, ahead, pa, pb, pc,
    left, right, values,
):
    dense[VOX:, :] = jnp.zeros((ROWS - VOX, MERGE), F32)
    for line in range(PLANE):
        dense[line * WIN : (line + 1) * WIN, :] = feats[line]
    hat = merged_norm(dense[...])
    normed = hat * hidden_rows(merge, 0, 1) + hidden_rows(merge, 4, 1)
    tokens = mm(normed, merge[8 : 8 + MERGE, :])
    tok0[...] = tokens
    layer = Rows(lay0, 0)
    normed = norm(tokens, layer[0:1, :], layer[1:2, :])
    attended = attention(normed, layer, save, lse, mixed, left, right, values)
    mid = tokens + attended
    middle[...] = mid
    tokens = mlp(mid, layer, hpre)
    tok1[...] = tokens
    ahead[...] = norm(tokens, lay1[1:2, :], lay1[2:3, :])
    send_parts(ahead, pa, pb, pc)


def shifted_kernel(
    own, pa, pb, pc, lay1, region_rows, region_lanes,
    window, save, lse, mixed, out, qa, qb, qc,
    left, right, values,
):
    take_parts(own, pa, pb, pc, window)
    out[...] = attention(
        window[...], Rows(lay1, 1), save, lse, mixed, left, right, values,
        (region_rows, region_lanes),
    )
    send_parts(out, qa, qb, qc)


def to_lines(ref, out):
    for line in range(PLANE):
        out[line, 0:WIN, :] = ref[line * WIN : (line + 1) * WIN, :]
        out[line, WIN:8, :] = jnp.zeros((8 - WIN, WIDE), F32)


def from_lines(ref, out):
    out[VOX:, :] = jnp.zeros((ROWS - VOX, WIDE), F32)
    for line in range(PLANE):
        out[line * WIN : (line + 1) * WIN, :] = ref[line, 0:WIN, :]


def second_kernel(
    tok1, own, qa, qb, qc, lay1, lay2,
    mid1, hpre1, tok2, save, lse, mixed, mid2, hpre2, lines,
    attended, left, right, values,
):
    take_parts(own, qa, qb, qc, attended)
    mid = tok1[...] + attended[...]
    mid1[...] = mid
    tokens = mlp(mid, Rows(lay1, 1), hpre1)
    tok2[...] = tokens
    layer = Rows(lay2, 2)
    normed = norm(tokens, layer[0:1, :], layer[1:2, :])
    mid = tokens + attention(normed, layer, save, lse, mixed, left, right, values)
    mid2[...] = mid
    attended[...] = mlp(mid, layer, hpre2)
    to_lines(attended, lines)


def grown_lines(own, low_d, high_d, low_h, high_h, out):
    out[...] = jnp.zeros_like(out)
    for d in range(WIN):
        out[d + 2, 2 : 2 + WIN] = own[d * WIN : (d + 1) * WIN]
    for d in range(2):
        out[d, 2 : 2 + WIN] = low_d[d * WIN : (d + 1) * WIN]
        out[d + 9, 2 : 2 + WIN] = high_d[d * WIN : (d + 1) * WIN]
    for d in range(11):
        out[d, 0:2] = low_h[2 * d : 2 * d + 2]
        out[d, 9:11] = high_h[2 * d : 2 * d + 2]


def taps(source, first_plane, planes, first_line, lines, out):
    def per_plane(d, carry):
        for c in range(3):
            for b in range(3):
                x = source[d + first_plane, first_line + b : first_line + b + lines]
                if c != 1:
                    x = roll(x, 1 if c == 0 else 7, 1)
                x = pair(x.reshape(lines * 8, WIDE))
                at = pl.multiple_of(d * (lines * 8), lines * 8)
                t = b * 3 + c
                out[pl.ds(at, lines * 8), t * 256 : (t + 1) * 256] = x
        return carry

    lax.fori_loop(0, planes, per_plane, 0)


def tap_weights(ref, at, out):
    def per_tap(i, carry):
        w = deep(ref[pl.ds(i * EMB + at, EMB), :])
        out[pl.ds(pl.multiple_of(i * 256, 256), 256), :] = weight_nn(w)
        return carry

    lax.fori_loop(0, 27, per_tap, 0)


def tap_weights_back(ref, at, out):
    def per_tap(i, carry):
        w = deep(ref[pl.ds((26 - i) * EMB + at, EMB), :]).T
        out[pl.ds(pl.multiple_of(i * 256, 256), 256), :] = weight_nn(w)
        return carry

    lax.fori_loop(0, 27, per_tap, 0)


def conv(side, weights, planes, pitch, at_once, put):
    rows = at_once * pitch
    for start in range(0, planes, at_once):
        total = None
        for a in range(3):
            low = (start + a) * pitch
            part = dot(side[low : low + rows, :], weights[a * 2304 : (a + 1) * 2304, :])
            total = part if total is None else total + part
        put(start, fold(total))


def conv_weight_grad(side, grad_rows, pitch, out, at):
    rows = 512
    g = jnp.concatenate([grad_rows, jnp.zeros((rows - grad_rows.shape[0], WIDE), F32)], 0)
    left = rows_t(g)
    for a in range(3):
        for bc in range(9):
            y = dot(left, side[a * pitch : a * pitch + rows, bc * 256 : (bc + 1) * 256])
            y = fold_rows(fold(y)).T
            t = a * 9 + bc
            out[at + t * EMB : at + (t + 1) * EMB, :] = y[:EMB]


def volume_mask(ends, planes, lines, reach, real_lines):
    shape = (planes, lines, 8, WIDE)
    d, h, w = iota(shape, 0), iota(shape, 1), iota(shape, 2)
    low_d = jnp.where(ends[0] == 1, reach, 0)
    high_d = jnp.where(ends[1] == 1, planes - reach, planes)
    low_h = jnp.where(ends[2] == 1, reach, 0)
    high_h = jnp.where(ends[3] == 1, real_lines - reach, real_lines)
    inside = (d >= low_d) & (d < high_d) & (h >= low_h) & (h < high_h) & (w < WIN)
    return jnp.where(inside, 1.0, 0.0)


def conv_kernel(
    ends, own, low_d, high_d, low_h, high_h, marks, conv0, conv1,
    grown, pre, tok, stats,
    act, side, side_own, weights,
):
    grown_lines(own, low_d, high_d, low_h, high_h, grown)
    tap_weights(conv0, 3, weights)
    taps(grown, 0, 11, 0, 10, side)
    bias0 = conv0[3 + TAP_ROWS : 4 + TAP_ROWS, :]
    inside = volume_mask(ends, 9, 10, 1, 9)

    def put(start, y):
        z = (y + bias0).reshape(3, 10, 8, WIDE)
        pre[start : start + 3] = z
        act[start : start + 3] = gelu(z) * inside[start : start + 3]

    conv(side, weights, 9, 80, 3, put)
    tap_weights(conv1, 0, weights)
    taps(act, 0, 9, 0, 8, side_own)
    bias1 = conv1[TAP_ROWS : TAP_ROWS + 1, :]
    sums = []

    def put_own(start, y):
        y = (y + bias1).reshape(WIN, 8, 8, WIDE)[:, 0:WIN]
        y = y + own[...].reshape(WIN, WIN, 8, WIDE)
        y = jnp.where(iota(y.shape, 2) < WIN, y, 0.0).reshape(PLANE, 8, WIDE)
        tok[...] = y + marks[...]
        flat = y.reshape(PLANE * 8, WIDE)
        sums.append(colsum(flat))
        sums.append(colsum(flat * flat))

    conv(side_own, weights, WIN, 64, WIN, put_own)
    count = jnp.sum(marks[...].reshape(PLANE * 8, WIDE))
    row = iota((8, WIDE), 0)
    stats[...] = (
        jnp.where(row == 0, sums[0], 0.0)
        + jnp.where(row == 1, sums[1], 0.0)
        + jnp.where(row == 2, count, 0.0)
    )


def head_kernel(
    own, low_d, high_d, low_h, high_h, sums, conv1, head_w, head_b, voxels,
    grown, slope_out, stats, d_head, d_rows,
):
    grown_lines(own, low_d, high_d, low_h, high_h, grown)
    rows = 11 * 12 * 8
    both = grown[...].reshape(rows, WIDE)
    lane = iota((rows, WIDE), 1)
    tokens = jnp.where(lane < EMB, both, 0.0)
    target = jnp.where(lane < CLASSES, roll(both, WIDE - EMB, 1), 0.0)
    live = jnp.sum(target, 1, keepdims=True)
    count = voxels[0]
    average = sums[0:1, :] / count
    spread = sums[1:2, :] / count - average * average
    inv = lax.rsqrt(spread + eps_norm)
    gain = conv1[TAP_ROWS + 1 : TAP_ROWS + 2, :]
    bias = conv1[TAP_ROWS + 2 : TAP_ROWS + 3, :]
    hat = (tokens - average) * inv
    act, slope = gelu_both(hat * gain + bias)
    w = head_w[...]
    logits = mm(act, w) + head_b[0:1, :]
    logits = jnp.where(lane < CLASSES, logits, -1e30)
    top = jnp.max(logits, 1, keepdims=True)
    e = jnp.exp(logits - top)
    total = jnp.sum(e, 1, keepdims=True)
    logp = logits - top - jnp.log(total)
    scale = 1.0 / sums[2:3, 0:1]
    d_logits = (e / total * live - target) * scale
    d_normed = mm_nt(d_logits, w) * slope
    d_tokens = d_normed * gain * inv
    slope_out[...] = d_tokens.reshape(11, 12, 8, WIDE)

    def own_rows(x):
        x = x.reshape(11, 12, 8, WIDE)[2:9, 2:9]
        x = jnp.where(iota(x.shape, 2) < WIN, x, 0.0)
        return x.reshape(PLANE * 8, WIDE)

    loss = -jnp.sum(own_rows(target * jnp.where(lane < CLASSES, logp, 0.0)))
    own_d = own_rows(d_logits)
    own_n = own_rows(d_normed)
    own_hat = own_rows(hat)
    zeros = jnp.zeros((512 - PLANE * 8, WIDE), F32)
    left = rows_t(jnp.concatenate([own_d, zeros], 0))
    d_head[...] = mm_tn(left, jnp.concatenate([own_rows(act), zeros], 0)).T
    d_gain = colsum(own_n * own_hat)
    d_bias = colsum(own_n)
    d_average = -d_bias * gain * inv
    d_spread = d_gain * gain * inv * inv * -0.5
    d_two = d_spread / count
    d_one = (d_average - 2.0 * average * d_spread) / count
    row = iota((8, WIDE), 0)
    live_lane = iota((8, WIDE), 1) < EMB
    stats[...] = (
        jnp.where((row == 0) & live_lane, d_one, 0.0)
        + jnp.where((row == 1) & live_lane, d_two, 0.0)
        + jnp.where(row == 2, loss, 0.0)
    )
    d_rows[...] = (
        jnp.where(row == 0, d_gain, 0.0)
        + jnp.where(row == 1, d_bias, 0.0)
        + jnp.where(row == 2, colsum(own_d), 0.0)
    )


def conv_back_kernel(
    ends, tok, slope, sums, grown, pre, conv0, conv1, d_rows, d_head,
    d_own, flat, carry,
    grads, dgrown, act, side, side_own, weights,
):
    lane = iota((11, 12, 8, WIDE), 3)
    inside = volume_mask(ends, 11, 12, 2, 11)
    steady = sums[0:1, :].reshape(1, 1, 1, WIDE)
    rising = 2.0 * sums[1:2, :].reshape(1, 1, 1, WIDE)
    d_tok = slope[...] + jnp.where(lane < EMB, (steady + tok[...] * rising) * inside, 0.0)
    dgrown[...] = d_tok
    grads[5208:, :] = jnp.zeros((28, WIDE), F32)
    grads[0:8, :] = jnp.zeros((8, WIDE), F32)
    grads[5189:5191, :] = d_rows[0:2, :]
    grads[5191:5208, :] = d_head[0:17, :]
    own = dgrown[2:9, 2:10]
    line = iota(own.shape, 1)
    own = jnp.where(line < WIN, own, 0.0).reshape(WIN * 64, WIDE)
    grads[5188:5189, :] = colsum(own)

    near = volume_mask(ends, 9, 10, 1, 9)
    act[0:9] = gelu(pre[...]) * near
    act[9:10] = jnp.zeros((1, 10, 8, WIDE), F32)
    taps(act, 0, 10, 0, 8, side_own)
    conv_weight_grad(side_own, own, 64, grads, 2596)
    tap_weights_back(conv1, 0, weights)
    taps(dgrown, 0, 11, 0, 10, side)

    def put(start, y):
        _, s = gelu_both(pre[start : start + 3])
        z = y.reshape(3, 10, 8, WIDE) * s * near[start : start + 3]
        act[start : start + 3] = z

    conv(side, weights, 9, 80, 3, put)

    own = act[1:8, 1:9]
    line = iota(own.shape, 1)
    own = jnp.where(line < WIN, own, 0.0).reshape(WIN * 64, WIDE)
    grads[2595:2596, :] = colsum(own)
    taps(grown, 1, 10, 1, 8, side_own)
    conv_weight_grad(side_own, own, 64, grads, 3)
    carry[...] = grads[0:24, :]
    flatten(grads, 20, GROUPS - CUTS[3], flat)
    tap_weights_back(conv0, 3, weights)
    taps(act, 0, 9, 0, 8, side_own)

    def put_own(start, y):
        y = y.reshape(WIN, 8, 8, WIDE)[:, 0:WIN] + dgrown[2:9, 2:9]
        y = jnp.where(iota(y.shape, 2) < WIN, y, 0.0)
        d_own[...] = y.reshape(PLANE, 8, WIDE)

    conv(side_own, weights, WIN, 64, WIN, put_own)


def back_two_kernel(
    d_own, carry, lay1, lay2, tok2, save, lse, mixed, mid2, hpre2, mid1, hpre1,
    d_mid, grads1, flat, carry2, pa, pb, pc,
    grads, dense, *sc,
):
    from_lines(d_own, dense)
    layer = Rows(lay2, 2)
    grads[0:8, :] = jnp.zeros((8, WIDE), F32)
    d = mlp_back(dense[...], mid2[...], hpre2, layer, grads, 2)
    tokens = tok2[...]
    normed = norm(tokens, layer[0:1, :], layer[1:2, :])
    d_normed = attention_back(d, normed, layer, save, lse, mixed, sc, grads, 2)
    d = d + pre_norm_back(d_normed, tokens, layer, grads, 2)
    grads[1167:1184, :] = carry[3:20, :]
    flatten(grads, 32, CUTS[3] - CUTS[2], flat)
    carry2[...] = grads[0:32, :]
    layer = Rows(lay1, 1)
    d = mlp_back(d, mid1[...], hpre1, layer, grads1, 1)
    d_mid[...] = d
    send_parts(d_mid, pa, pb, pc)


def back_shifted_kernel(
    own, pa, pb, pc, lay1, region_rows, region_lanes, window, save, lse, mixed, grads1, carry2,
    d_window, flat, carry1, qa, qb, qc,
    grads, grad, *sc,
):
    take_parts(own, pa, pb, pc, grad)
    grads[0:1168, :] = grads1[...]
    grads[0:3, :] = jnp.zeros((3, WIDE), F32)
    d_window[...] = attention_back(
        grad[...], window[...], Rows(lay1, 1), save, lse, mixed, sc, grads, 1,
        (region_rows, region_lanes),
    )
    send_parts(d_window, qa, qb, qc)
    grads[1166:1196, :] = carry2[2:32, :]
    flatten(grads, 12, CUTS[2] - CUTS[1], flat)
    carry1[...] = grads[0:16, :]


def back_first_kernel(
    d_mid, own, qa, qb, qc, tok1, lay0, lay1, merge, dense, tok0, save, lse, mixed, middle, hpre, carry1,
    flat,
    grads, grad, *sc,
):
    take_parts(own, qa, qb, qc, grad)
    grads[1556:1572, :] = carry1[...]
    d = d_mid[...] + pre_norm_back(grad[...], tok1[...], Rows(lay1, 1), grads, 1557)
    layer = Rows(lay0, 0)
    at = MERGE_ROWS
    d = mlp_back(d, middle[...], hpre, layer, grads, at)
    tokens = tok0[...]
    normed = norm(tokens, layer[0:1, :], layer[1:2, :])
    d_normed = attention_back(d, normed, layer, save, lse, mixed, sc, grads, at)
    d = d + pre_norm_back(d_normed, tokens, layer, grads, at)
    live = iota((ROWS, WIDE), 0) < VOX
    d = jnp.where(live, d, 0.0)
    hat = merged_norm(dense[...])
    gain = hidden_rows(merge, 0, 1)
    bias = hidden_rows(merge, 4, 1)
    w = merge[8 : 8 + MERGE, :]
    put_hidden_rows(grads, 8 - 8, 1, jnp.zeros((1, MERGE), F32))
    grads[8 : 8 + MERGE, :] = mm_tn(rows_t(d), hat * gain + bias).T
    d_hat = mm_nt(d, w)
    put_hidden_rows(grads, 0, 1, colsum(d_hat * hat))
    put_hidden_rows(grads, 4, 1, colsum(d_hat))
    flatten(grads, 0, CUTS[1], flat)


def arr(*shape):
    return jax.ShapeDtypeStruct(shape, F32)


def call(kernel, outs, scratch, *args, scalars=0, name=None):
    smem = pl.BlockSpec(memory_space=pltpu.SMEM)
    vmem = pl.BlockSpec(memory_space=pltpu.VMEM)
    specs = [smem if a.size <= 8 and a.ndim == 1 else vmem for a in args]
    return pl.pallas_call(
        kernel,
        out_shape=list(outs),
        in_specs=specs,
        out_specs=[vmem] * len(outs),
        scratch_shapes=list(scratch),
        compiler_params=pltpu.CompilerParams(vmem_limit_bytes=VMEM),
        name=name,
    )(*args)


SQUARE = arr(ROWS, WIDE)
SAVE = arr(ROWS, 3 * WIDE)
FORWARD = [
    pltpu.VMEM((2, ROWS, 2 * WIDE), BF16),
    pltpu.VMEM((2, ROWS, 2 * WIDE), BF16),
    pltpu.VMEM((2 * ROWS, 2 * WIDE), BF16),
]
BACKWARD = [
    pltpu.VMEM((2, ROWS, 2 * WIDE), BF16),
    pltpu.VMEM((2, ROWS, 2 * WIDE), BF16),
    pltpu.VMEM((2, ROWS, 2 * WIDE), BF16),
    pltpu.VMEM((2, ROWS, 2 * WIDE), BF16),
    pltpu.VMEM((2 * ROWS, 2 * WIDE), BF16),
    pltpu.VMEM((ROWS, WIDE), F32),
    pltpu.VMEM((2, WIDE, ROWS), F32),
    pltpu.VMEM((ROWS, 2 * ROWS), BF16),
    pltpu.VMEM((ROWS, 2 * ROWS), BF16),
    pltpu.VMEM((2, WIDE, ROWS), BF16),
    pltpu.VMEM((2, WIDE, ROWS), BF16),
    pltpu.VMEM((ROWS, WIDE), F32),
]
PARTS = [arr(ROWS_A, WIDE), arr(ROWS_B, WIDE), arr(ROWS_C, WIDE)]


def passed(parts, steps, sizes):
    slabs, rows = sizes
    moved = []
    for part, (ds, dm) in zip(parts, ((1, 0), (0, 1), (1, 1))):
        pairs = []
        for s in range(slabs):
            for m in range(rows):
                target = ((s + steps * ds) % slabs) * rows + (m + steps * dm) % rows
                pairs.append((s * rows + m, target))
        moved.append(lax.ppermute(part, ("slab", "mp"), pairs))
    return moved


def beside(lines, sizes):
    slabs, rows = sizes
    up = [(i, i + 1) for i in range(slabs - 1)]
    down = [(i + 1, i) for i in range(slabs - 1)]
    low_d = lax.ppermute(lines[(WIN - 2) * WIN :], "slab", up)
    high_d = lax.ppermute(lines[: 2 * WIN], "slab", down)
    column = jnp.concatenate([low_d, lines, high_d], 0).reshape(11, WIN, 8, WIDE)
    first = column[:, 0:2].reshape(22, 8, WIDE)
    last = column[:, WIN - 2 :].reshape(22, 8, WIDE)
    up = [(i, i + 1) for i in range(rows - 1)]
    down = [(i + 1, i) for i in range(rows - 1)]
    low_h = lax.ppermute(last, "mp", up)
    high_h = lax.ppermute(first, "mp", down)
    return low_d, high_d, low_h, high_h


def window_regions(slab, row, sizes):
    def part_of(places, length):
        return jnp.where(places < length - WIN, 0, jnp.where(places < length - SHIFT, 1, 2))

    turned = (jnp.arange(WIN, dtype=jnp.int32) + FAR) % WIN
    depth = part_of(slab * WIN + turned, WIN * sizes[0])
    height = part_of(row * WIN + turned, WIN * sizes[1])
    breadth = part_of(turned, WIN)
    ids = depth[:, None, None] * 9 + height[None, :, None] * 3 + breadth[None, None, :]
    ids = jnp.pad(ids.reshape(VOX).astype(F32), (0, ROWS - VOX))
    return jnp.broadcast_to(ids[:, None], (ROWS, WIDE)), jnp.broadcast_to(ids[None], (8, ROWS))


def adamw(param, grad, first, second, scale):
    grad = grad * scale
    first = beta_one * first + (1.0 - beta_one) * grad
    second = beta_two * second + (1.0 - beta_two) * grad * grad
    first_hat = first / (1.0 - beta_one**STEP)
    second_hat = second / (1.0 - beta_two**STEP)
    param = param - learn_rate * (
        first_hat / (jnp.sqrt(second_hat) + adam_eps) + decay_rate * param
    )
    return (param, first, second)


def on_device(sizes, feats, labels, valid, params, moment_one, moment_two):
    slabs, rows = sizes
    slab, row = lax.axis_index("slab"), lax.axis_index("mp")
    both = ("slab", "mp")
    ends = jnp.stack([slab == 0, slab == slabs - 1, row == 0, row == rows - 1]).astype(jnp.int32)
    region = window_regions(slab, row, sizes)
    voxels = jnp.full((1,), WIN * slabs * WIN * rows * WIN, F32)

    flat = jnp.pad(params, (0, FLAT_ROWS * WIDE - NPARAM)).reshape(FLAT_ROWS, WIDE)
    merge, lay0, lay1, lay2, conv0, conv1 = call(
        prep_kernel,
        [arr(MERGE_ROWS, WIDE)] + [arr(1168, WIDE)] * 3 + [arr(2596, WIDE), arr(2640, WIDE)],
        [],
        flat,
        name="prep",
    )
    head = params[NPARAM - CLASSES * (EMB + 1) :]
    head_w = jnp.pad(
        head[: EMB * CLASSES].reshape(EMB, CLASSES), ((0, WIDE - EMB), (0, WIDE - CLASSES))
    )
    head_b = jnp.broadcast_to(jnp.pad(head[EMB * CLASSES :], (0, WIDE - CLASSES)), (8, WIDE))
    classes = jnp.arange(WIDE, dtype=jnp.int32) - EMB
    marks = (labels[..., None] == classes).astype(F32) * valid.astype(F32)[..., None]
    marks = jnp.pad(marks, ((0, 0), (0, 0), (0, 1), (0, 0))).reshape(PLANE, 8, WIDE)

    dense, tok0, save0, lse0, mixed0, mid0, hpre0, tok1, ahead, *parts = call(
        first_kernel,
        [arr(ROWS, MERGE), SQUARE, SAVE, SQUARE, SQUARE, SQUARE, arr(ROWS, HID), SQUARE, SQUARE]
        + PARTS,
        FORWARD,
        feats.reshape(PLANE, WIN, MERGE), merge, lay0, lay1,
        name="first",
    )
    parts = passed(parts, -1, sizes)
    window, save1, lse1, mixed1, out1, *parts = call(
        shifted_kernel,
        [SQUARE, SAVE, SQUARE, SQUARE, SQUARE] + PARTS,
        FORWARD,
        ahead, *parts, lay1, *region,
        name="shifted",
    )
    parts = passed(parts, 1, sizes)
    mid1, hpre1, tok2, save2, lse2, mixed2, mid2, hpre2, lines = call(
        second_kernel,
        [SQUARE, arr(ROWS, HID), SQUARE, SAVE, SQUARE, SQUARE, SQUARE, arr(ROWS, HID)]
        + [arr(PLANE, 8, WIDE)],
        [pltpu.VMEM((ROWS, WIDE), F32)] + FORWARD,
        tok1, out1, *parts, lay1, lay2,
        name="second",
    )
    near = beside(lines, sizes)
    grown, pre, tok3, stats = call(
        conv_kernel,
        [arr(11, 12, 8, WIDE), arr(9, 10, 8, WIDE), arr(PLANE, 8, WIDE), arr(8, WIDE)],
        [
            pltpu.VMEM((9, 10, 8, WIDE), F32),
            pltpu.VMEM((880, 2304), BF16),
            pltpu.VMEM((576, 2304), BF16),
            pltpu.VMEM((27 * 256, 256), BF16),
        ],
        ends, lines, *near, marks, conv0, conv1,
        name="conv",
    )
    near = beside(tok3, sizes)
    stats = lax.psum(stats, both)
    tok3, slope, tail, d_head, d_rows = call(
        head_kernel,
        [arr(11, 12, 8, WIDE), arr(11, 12, 8, WIDE), arr(8, WIDE), arr(WIDE, WIDE), arr(8, WIDE)],
        [],
        tok3, *near, stats, conv1, head_w, head_b, voxels,
        name="head",
    )
    d_head = jnp.concatenate([d_head[:EMB, :CLASSES].reshape(-1), d_rows[2, :CLASSES]])
    d_head = jnp.pad(d_head, (0, 24 * EMB - CLASSES * (EMB + 1))).reshape(24, EMB)
    d_head = jnp.pad(d_head, ((0, 0), (0, WIDE - EMB)))
    tail = lax.psum(tail, both)
    d_own, flat3, carry3 = call(
        conv_back_kernel,
        [arr(PLANE, 8, WIDE), arr(3 * (CUTS[4] - CUTS[3]), WIDE), arr(24, WIDE)],
        [
            pltpu.VMEM((5236, WIDE), F32),
            pltpu.VMEM((11, 12, 8, WIDE), F32),
            pltpu.VMEM((10, 10, 8, WIDE), F32),
            pltpu.VMEM((880, 2304), BF16),
            pltpu.VMEM((640, 2304), BF16),
            pltpu.VMEM((27 * 256, 256), BF16),
        ],
        ends, tok3, slope, tail, grown, pre, conv0, conv1, d_rows, d_head,
        name="conv_back",
    )
    flat3 = lax.psum(flat3.reshape(-1), both)
    d_mid, grads1, flat2, carry2, *parts = call(
        back_two_kernel,
        [SQUARE, arr(1168, WIDE), arr(3 * (CUTS[3] - CUTS[2]), WIDE), arr(32, WIDE)] + PARTS,
        [pltpu.VMEM((1184, WIDE), F32), pltpu.VMEM((ROWS, WIDE), F32)] + BACKWARD,
        d_own, carry3, lay1, lay2, tok2, save2, lse2, mixed2, mid2, hpre2, mid1, hpre1,
        name="back_two",
    )
    flat2 = lax.psum(flat2.reshape(-1), both)
    parts = passed(parts, -1, sizes)
    d_window, flat1, carry1, *parts = call(
        back_shifted_kernel,
        [SQUARE, arr(3 * (CUTS[2] - CUTS[1]), WIDE), arr(16, WIDE)] + PARTS,
        [pltpu.VMEM((1200, WIDE), F32), pltpu.VMEM((ROWS, WIDE), F32)] + BACKWARD,
        d_mid, *parts, lay1, *region, window, save1, lse1, mixed1, grads1, carry2,
        name="back_shifted",
    )
    flat1 = lax.psum(flat1.reshape(-1), both)
    parts = passed(parts, 1, sizes)
    (flat0,) = call(
        back_first_kernel,
        [arr(3 * (CUTS[1] - CUTS[0]), WIDE)],
        [pltpu.VMEM((1572, WIDE), F32), pltpu.VMEM((ROWS, WIDE), F32)] + BACKWARD,
        d_mid, d_window, *parts, tok1, lay0, lay1, merge, dense, tok0, save0, lse0, mixed0, mid0,
        hpre0, carry1,
        name="back_first",
    )
    flat0 = lax.psum(flat0.reshape(-1), both)
    gradient = jnp.concatenate([flat0, flat1, flat2, flat3])[:NPARAM]
    grad_norm = jnp.sqrt(jnp.sum(gradient * gradient))
    scale = jnp.minimum(1.0, clip_norm / (grad_norm + 1e-06))
    new_params, new_first, new_second = adamw(params, gradient, moment_one, moment_two, scale)
    return (tail[2, 0], stats[2, 0], grad_norm, new_params, new_first, new_second)


def solution(mesh):
    placed = (
        P("slab", "mp", None, None),
        P("slab", "mp", None),
        P("slab", "mp", None),
        P(),
        P(),
        P(),
    )
    sizes = (mesh.shape["slab"], mesh.shape["mp"])
    return jax.shard_map(
        functools.partial(on_device, sizes),
        mesh=mesh,
        in_specs=placed,
        out_specs=(P(), P(), P(), P(), P(), P()),
        check_vma=False,
    )
```

time: 824 us -> 447 us (0.54)
  matrix products: 232 us -> 0 us
  other arithmetic: 137 us -> 16.7 us
  local copies, waits for them, and re-layouts: 130 us -> 21.8 us
  Pallas kernels: 0 us -> 105 us
  starting transfers between devices: 51.6 us -> 37 us
    dot_general x222 -> x0, matrix products: 232 us -> none  [the longest x204 169 us: matmul(): return jnp.einsum('...c,cd->...d', tokens, weight, precision=HIGH)]
    pallas_call x0 -> x10, Pallas kernels: none -> 105 us  [call(): pl.pallas_call(kernel, out_shape=list(outs), in_specs=specs, out_specs=[v...]
    add x6 -> x1, other arithmetic: 65.4 us -> 0.07 us  [window_regions(): depth[:, None, None] * 9 + height[None, :, None] * 3]
    reshape x36 -> x4, local copies, waits for them, and re-layouts: 48.6 us -> 5.6 us  [the longest x1 3.94 us: on_device(): jnp.pad(params, (0, FLAT_ROWS * WIDE - NPARAM)).reshape(FLAT_ROWS, WIDE)]
    reduce_sum x39 -> x0, other arithmetic: 34.8 us -> none  [the longest x9 10.5 us: norm_rows(): return centred * lax.rsqrt(spread + eps_norm) * gain_row + bias_row]
    slice x34 -> x9, local copies, waits for them, and re-layouts: 35.5 us -> 7.13 us  [the longest x2 2.5 us: beside(): high_d = lax.ppermute(lines[:2 * WIN], 'slab', down)]
    ppermute x24 -> x20, starting transfers between devices: 51.5 us -> 36.9 us  [the longest x12 16.3 us: passed(): moved.append(lax.ppermute(part, ('slab', 'mp'), pairs))]
    unnamed x428 -> x38, local copies, waits for them, and re-layouts: 12.7 us -> 2.54 us
  transfers between devices with their start and end apart: 25 -> 21, of which waited for: 8 -> 10; matrix products, arithmetic and copies ran while one was open for 12% -> 2% of each run, Pallas kernels for 0% -> 0%
where the time goes in v1:
time: 447 us; the launch traced here: 439 us
  waiting for transfers between devices  160 us (36%)
  Pallas kernels  105 us (23%)
  blocking collectives  82.8 us (19%)
  starting transfers between devices  37 us (8%)
  local copies, waits for them, and re-layouts  21.8 us (5%)
  other arithmetic  16.7 us (4%)
  between operations  16.5 us (4%)
    psum x1, waiting for transfers between devices, on_device(): flat3 = lax.psum(flat3.reshape(-1), both)  137 us
    pallas_call x10, Pallas kernels, call(): pl.pallas_call(kernel, out_shape=list(outs), in_specs=specs, out_specs=[v...  105 us
    psum x1, blocking collectives, on_device(): stats = lax.psum(stats, both)  41.9 us
    psum x1, blocking collectives, on_device(): tail = lax.psum(tail, both)  40.9 us
    ppermute x12, waiting for transfers between devices, passed(): moved.append(lax.ppermute(part, ('slab', 'mp'), pairs))  17.9 us
    ppermute x12, starting transfers between devices, passed(): moved.append(lax.ppermute(part, ('slab', 'mp'), pairs))  16.3 us
    ppermute x2, starting transfers between devices, beside(): low_d = lax.ppermute(lines[(WIN - 2) * WIN:], 'slab', up)  9.71 us
  transfers between devices with their start and end apart: 21, of which 10 were waited for; matrix products, arithmetic and copies ran while one was open for 2% of the time, Pallas kernels for 0%

profile of v1, /device:TPU:0, one launch (start us, length us, event | category | flops | bytes accessed | tf_op | source)
XLA Modules:
  0.0 439.2 jit_solution(12563027379410608363)
XLA Ops:
  7.2 3.9 pad_bitcast_fusion.flat
  11.2 4.7 %prep.1 = (f32[392,128]{1,0:T(8,128)}, f32[1168,128]{1,0:T(8,128)}, f32[1168,128]{1,0:T(8,128)}, f32[1168,128]{1,0:T(8,128)}, f32[2596,128]{1,0:T(8,128)}, /*index=5*/f32[2640,128]{1,0:T(8,128)}) custom-call(f32[6840,128]{1,0:T(8,128)} %pad_bitcast_fusion.flat), custom_call_target="tpu_custom_call" | custom-call | tf_op jit(solution)/shard_map/prep/pallas_call | solution.py:818
  15.8 9.5 %first.1 = (f32[384,384]{1,0:T(8,128)}, f32[384,128]{1,0:T(8,128)}, f32[384,384]{1,0:T(8,128)}, f32[384,128]{1,0:T(8,128)}, f32[384,128]{1,0:T(8,128)}, /*index=...) custom-call(f32[49,7,384]{2,1,0:T(8,128)} %bitcast.27, ...), custom_call_target="tpu_custom_call" | custom-call | tf_op jit(solution)/shard_map/first/pallas_call | solution.py:818
  25.3 6.4 %collective-permute-start.2 = (f32[63,128]{1,0:T(8,128)}, f32[63,128]{1,0:T(8,128)S(1)}, u32[]{:S(2)}, u32[]{:S(2)}) collective-permute-start(f32[63,128]{1,0:T(8,128)} %get-tuple-element.73), channel_id=1, source_target_pairs={{0,31},{1,28},{2,29},{3,30},{4,3},{5,0},{6,1},{7,2},{8,7},{9,4},{1... | collective-permute-start | bytes 96776 | tf_op jit(solution)/shard_map/ppermute | solution.py:862
  33.6 2.3 collective-permute-done.pa
  36.6 0.8 broadcast_in_dim.39.region_rows
  37.4 7.4 %shifted.1 = (f32[384,128]{1,0:T(8,128)}, f32[384,384]{1,0:T(8,128)}, f32[384,128]{1,0:T(8,128)}, f32[384,128]{1,0:T(8,128)}, f32[384,128]{1,0:T(8,128)}, /*inde...) custom-call(f32[384,128]{1,0:T(8,128)} %get-tuple-element.70.own, f32[84,128]{1,0:T(8,128)} %copy-done.8, ...), custom_call_target="tpu_custom_call" | custom-call | tf_op jit(solution)/shard_map/shifted/pallas_call | solution.py:818
  45.5 6.5 %collective-permute-done.5.qc = f32[63,128]{1,0:T(8,128)S(1)} collective-permute-done((f32[63,128]{1,0:T(8,128)}, f32[63,128]{1,0:T(8,128)S(1)}, u32[]{:S(2)}, u32[]{:S(2)}) %collective-permute-start.5) | collective-permute-done | bytes 32288 | tf_op jit(solution)/shard_map/ppermute | solution.py:862
  52.9 9.6 %second.1 = (f32[384,128]{1,0:T(8,128)}, f32[384,384]{1,0:T(8,128)}, f32[384,128]{1,0:T(8,128)}, f32[384,384]{1,0:T(8,128)}, f32[384,128]{1,0:T(8,128)}, /*index...) custom-call(f32[384,128]{1,0:T(8,128)} %get-tuple-element.69.tok1, ...), custom_call_target="tpu_custom_call" | custom-call | tf_op jit(solution)/shard_map/second/pallas_call | solution.py:818
  62.4 1.6 fusion.7
  64.1 1.3 collective-permute-start.7
  65.4 5.2 %collective-permute-start.6 = (f32[14,8,128]{2,1,0:T(8,128)}, f32[14,8,128]{2,1,0:T(8,128)}, u32[]{:S(2)}, u32[]{:S(2)}) collective-permute-start(f32[14,8,128]{2,1,0:T(8,128)} %get-tuple-element.140), channel_id=1, source_target_pairs={{0,4},{4,8},{8,12},{12,16},{16,20},{20,24},{24,28},{1,5},{5,9},{9,... | collective-permute-start | bytes 172040 | tf_op jit(solution)/shard_map/ppermute | solution.py:870
  70.5 1.6 compare_select_fusion
  72.1 1.6 pad.30
  73.8 1.0 pad_maximum_fusion.3
  74.8 1.3 collective-permute-start.8
  76.1 1.5 collective-permute-start.9
  78.2 2.8 collective-permute-done.9.high_h
  81.6 10.5 %conv.1 = (f32[11,12,8,128]{3,2,1,0:T(8,128)}, f32[9,10,8,128]{3,2,1,0:T(8,128)}, f32[49,8,128]{2,1,0:T(8,128)}, f32[8,128]{1,0:T(8,128)}) custom-call(s32[4]{0:T(128)} %add_convert_fusion.1.ends, f32[49,8,128]{2,1,0:T(8,128)} %get-tuple-element.79.own, f32[14,8,128]{2,1,0:T(8,128)} %collective-permute-done.6.low_d, f32[14,8,128]{2,1,0:T(8,128)} %copy-done.1, ...), custom_call_target="tpu_custom_call" | custom-call | tf_op jit(solution)/shard_map/conv/pallas_call | solution.py:818
  92.2 0.9 fusion.6
  93.0 1.3 collective-permute-start.11
  94.3 4.5 %collective-permute-start.10 = (f32[14,8,128]{2,1,0:T(8,128)S(1)}, f32[14,8,128]{2,1,0:T(8,128)S(1)}, u32[]{:S(2)}, u32[]{:S(2)}) collective-permute-start(f32[14,8,128]{2,1,0:T(8,128)S(1)} %get-tuple-element.138), channel_id=1, source_target_pairs={{0,4},{4,8},{8,12},{12,16},{16,20},{20,24},{24,28},{1,5},{5,9},{9,... | collective-permute-start | bytes 172040 | tf_op jit(solution)/shard_map/ppermute | solution.py:870
  99.1 1.9 collective-permute-done.10.low_d
  101.0 1.0 pad_maximum_fusion.4
  101.9 0.7 fusion.4
  102.6 4.3 collective-permute-start.12
  106.9 1.3 collective-permute-start.13
  108.9 1.4 reshape.162
  110.4 1.4 pad.31.head_w
  111.8 41.9 %psum.42.sums = f32[8,128]{1,0:T(8,128)} all-reduce(f32[8,128]{1,0:T(8,128)} %get-tuple-element.83), channel_id=1, replica_groups=mesh['slab'=8,'mp'=4] {'slab','mp'}, use_global_device_ids=true, to_apply=%region_0.1 | all-reduce | flops 1024 | bytes 8192 | tf_op jit(solution)/shard_map/psum | solution.py:971
  154.4 3.5 head.1
  157.9 40.9 %psum.43.sums = f32[8,128]{1,0:T(8,128)} all-reduce(f32[8,128]{1,0:T(8,128)} %get-tuple-element.84), channel_id=1, replica_groups=mesh['slab'=8,'mp'=4] {'slab','mp'}, use_global_device_ids=true, to_apply=%region_1.2 | all-reduce | flops 1024 | bytes 8192 | tf_op jit(solution)/shard_map/psum | solution.py:982
  199.5 0.8 slice.60
  201.2 21.1 %conv_back.1 = (f32[49,8,128]{2,1,0:T(8,128)}, f32[3912,128]{1,0:T(8,128)}, f32[24,128]{1,0:T(8,128)}) custom-call(s32[4]{0:T(128)} %add_convert_fusion.1.ends, f32[11,12,8,128]{3,2,1,0:T(8,128)} %get-tuple-element.85.tok, f32[11,12,8,128]{3,2,1,0:T(8,128)} %get-tuple-element.86.slope, f32[8,128]{1,0:T(8,128)} %psum.43.sums, ...), custom_call_target="tpu_custom_call" | custom-call | tf_op jit(solution)/shard_map/conv_back/pallas_call | solution.py:818
  222.2 14.3 %back_two.1 = (f32[384,128]{1,0:T(8,128)}, f32[1168,128]{1,0:T(8,128)}, f32[864,128]{1,0:T(8,128)}, f32[32,128]{1,0:T(8,128)}, f32[84,128]{1,0:T(8,128)}, /*index=5*/f32[84,128]{1,0:T(8,128)}, f32[63,128]{1,0:T(8,128)}) custom-call(f32[49,8,128]{2,1,0:T(8,128)} %get-tuple-element.91.d_own, f32[24,128]{1,0:T(8,128)} %get-tuple-element.92.carry, ...), custom_call_target="tpu_custom_call" | custom-call | tf_op jit(solution)/shard_map/back_two/pallas_call | solution.py:818
  236.5 4.0 collective-permute-start.14
  240.6 1.8 collective-permute-start.16
  242.4 1.9 collective-permute-done.16.pc
  245.0 10.6 %back_shifted.1 = (f32[384,128]{1,0:T(8,128)}, f32[888,128]{1,0:T(8,128)}, f32[16,128]{1,0:T(8,128)}, f32[84,128]{1,0:T(8,128)}, f32[84,128]{1,0:T(8,128)}, /*index=5*/f32[63,128]{1,0:T(8,128)}) custom-call(f32[384,128]{1,0:T(8,128)} %get-tuple-element.101.own.d_mid, f32[84,128]{1,0:T(8,128)} %copy-done.10, f32[84,128]{1,0:T(8,128)} %copy-done.11, ...), custom_call_target="tpu_custom_call" | custom-call | tf_op jit(solution)/shard_map/back_shifted/pallas_call | solution.py:818
  256.0 0.9 collective-permute-start.18
  256.9 1.0 collective-permute-start.19
  257.9 6.4 %collective-permute-done.19.qc = f32[63,128]{1,0:T(8,128)S(1)} collective-permute-done((f32[63,128]{1,0:T(8,128)}, f32[63,128]{1,0:T(8,128)S(1)}, u32[]{:S(2)}, u32[]{:S(2)}) %collective-permute-start.19) | collective-permute-done | bytes 32288 | tf_op jit(solution)/shard_map/ppermute | solution.py:862
  265.0 13.6 %back_first.1 = f32[1176,128]{1,0:T(8,128)} custom-call(f32[384,128]{1,0:T(8,128)} %get-tuple-element.101.own.d_mid, f32[384,128]{1,0:T(8,128)} %get-tuple-element.111.own, f32[84,128]{1,0:T(8,128)} %copy-done.6, f32[84,128]{1,0:T(8,128)} %copy-done.7, f32[63,128]{1,0:T(8,128)} %copy-done.15, f32[384,128]{1,0:T(8,128)} %get-tuple-element.69.tok1, ...), custom_call_target="tpu_custom_call" | custom-call | tf_op jit(solution)/shard_map/back_first/pallas_call | solution.py:818
  278.6 1.2 slice.59
  279.8 1.2 slice.58
  281.0 136.8 %all-reduce.10.cloned.1.call-done = (f32[500736]{0:T(1024)}, f32[110592]{0:T(1024)}, f32[113664]{0:T(1024)}, f32[150528]{0:T(1024)}) async-done(((f32[500736]{0:T(1024)}, f32[110592]{0:T(1024)}, f32[113664]{0:T(1024)}, f32[150528]{0:T(1024)}), (f32[500736]{0:T(1024)}, f32[110592]{0:T(1024)}, f32[113664]{0:T(1024)}, f32[150528]{0:T(1024)})) %all-reduce.10.cloned.1.call-update) | async-done | bytes 3502096 | tf_op jit(solution)/shard_map/psum | solution.py:997
  417.8 3.4 multiply_reduce_fusion
  422.0 8.8 %multiply_subtract_fusion = (f32[872558]{0:T(1024)}, f32[872558]{0:T(1024)}, f32[872558]{0:T(1024)}) fusion(f32[872558]{0:T(1024)S(1)} %copy-done, f32[]{:T(128)S(6)} %min_shard_map.3, f32[500736]{0:T(1024)} %get-tuple-element.126, f32[110592]{0:T(1024)} %get-tuple-element.127, f32[113664]{0:T(1024)} %get-tuple-element.128, f32[150528]{0:T(1024)} %get-tuple-element.129, ...), kind=kLoop, calls=%fused_computation.6 | loop fusion | flops 16578602 | bytes 24443476 | tf_op jit(solution)/shard_map/sub | solution.py:901
  (81 shorter events, 10.3 us)
Async XLA Ops:
  7.2 410.6 %all-reduce.10.cloned.1.call-start = ((), (), s32[]{:S(2)}) async-start(), calls=%async_computation | async-start | bytes 7004160 | tf_op jit(solution)/shard_map/psum | solution.py:997
  11.2 34.3 %copy-start.18 = (s32[7,7,7]{2,1,0:T(8,128)S(1)}, s32[7,7,7]{2,1,0:T(8,128)}, u32[]{:S(2)}) copy-start(s32[7,7,7]{2,1,0:T(8,128)} %param.8) | copy-start | bytes 4120
  25.3 8.3 %collective-permute-start.2 = (f32[63,128]{1,0:T(8,128)}, f32[63,128]{1,0:T(8,128)S(1)}, u32[]{:S(2)}, u32[]{:S(2)}) collective-permute-start(f32[63,128]{1,0:T(8,128)} %get-tuple-element.73), channel_id=1, source_target_pairs={{0,31},{1,28},{2,29},{3,30},{4,3},{5,0},{6,1},{7,2},{8,7},{9,4},{1... | collective-permute-start | bytes 96776 | tf_op jit(solution)/shard_map/ppermute | solution.py:862
  31.7 4.3 collective-permute-start
  32.2 3.7 collective-permute-start.1
  33.6 3.8 copy-start.16
  35.9 1.4 copy-start.8
  36.0 1.4 copy-start.9
  44.8 7.1 %collective-permute-start.5 = (f32[63,128]{1,0:T(8,128)}, f32[63,128]{1,0:T(8,128)S(1)}, u32[]{:S(2)}, u32[]{:S(2)}) collective-permute-start(f32[63,128]{1,0:T(8,128)} %get-tuple-element.77), channel_id=1, source_target_pairs={{0,5},{1,6},{2,7},{3,4},{4,9},{5,10},{6,11},{7,8},{8,13},{9,14},{1... | collective-permute-start | bytes 96776 | tf_op jit(solution)/shard_map/ppermute | solution.py:862
  45.3 7.0 %collective-permute-start.3 = (f32[84,128]{1,0:T(8,128)}, f32[84,128]{1,0:T(8,128)S(1)}, u32[]{:S(2)}, u32[]{:S(2)}) collective-permute-start(f32[84,128]{1,0:T(8,128)} %get-tuple-element.75), channel_id=1, source_target_pairs={{0,4},{1,5},{2,6},{3,7},{4,8},{5,9},{6,10},{7,11},{8,12},{9,13},{1... | collective-permute-start | bytes 129032 | tf_op jit(solution)/shard_map/ppermute | solution.py:862
  45.3 7.0 %collective-permute-start.4 = (f32[84,128]{1,0:T(8,128)}, f32[84,128]{1,0:T(8,128)S(1)}, u32[]{:S(2)}, u32[]{:S(2)}) collective-permute-start(f32[84,128]{1,0:T(8,128)} %get-tuple-element.76), channel_id=1, source_target_pairs={{0,1},{1,2},{2,3},{3,0},{4,5},{5,6},{6,7},{7,4},{8,9},{9,10},{10,1... | collective-permute-start | bytes 129032 | tf_op jit(solution)/shard_map/ppermute | solution.py:862
  51.9 0.6 copy-start.17
  52.2 0.6 copy-start.12
  52.2 0.6 copy-start.13
  62.4 45.8 %copy-start = (f32[872558]{0:T(1024)S(1)}, f32[872558]{0:T(1024)}, u32[]{:S(2)}) copy-start(f32[872558]{0:T(1024)} %param.9) | copy-start | bytes 10470700
  64.1 9.7 %collective-permute-start.7 = (f32[14,8,128]{2,1,0:T(8,128)}, f32[14,8,128]{2,1,0:T(8,128)S(1)}, u32[]{:S(2)}, u32[]{:S(2)}) collective-permute-start(f32[14,8,128]{2,1,0:T(8,128)} %get-tuple-element.139), channel_id=1, source_target_pairs={{4,0},{8,4},{12,8},{16,12},{20,16},{24,20},{28,24},{5,1},{9,5},{13... | collective-permute-start | bytes 172040 | tf_op jit(solution)/shard_map/ppermute | solution.py:871
  65.4 8.4 %collective-permute-start.6 = (f32[14,8,128]{2,1,0:T(8,128)}, f32[14,8,128]{2,1,0:T(8,128)}, u32[]{:S(2)}, u32[]{:S(2)}) collective-permute-start(f32[14,8,128]{2,1,0:T(8,128)} %get-tuple-element.140), channel_id=1, source_target_pairs={{0,4},{4,8},{8,12},{12,16},{16,20},{20,24},{24,28},{1,5},{5,9},{9,... | collective-permute-start | bytes 172040 | tf_op jit(solution)/shard_map/ppermute | solution.py:870
  73.8 7.2 %copy-start.1 = (f32[14,8,128]{2,1,0:T(8,128)}, f32[14,8,128]{2,1,0:T(8,128)S(1)}, u32[]{:S(2)}) copy-start(f32[14,8,128]{2,1,0:T(8,128)S(1)} %collective-permute-done.7.high_d) | copy-start | bytes 172036
  74.8 3.4 collective-permute-start.8
  76.1 4.9 %collective-permute-start.9 = (f32[22,8,128]{2,1,0:T(8,128)S(1)}, f32[22,8,128]{2,1,0:T(8,128)S(1)}, u32[]{:S(2)}, u32[]{:S(2)}) collective-permute-start(f32[22,8,128]{2,1,0:T(8,128)S(1)} %bitcast.30), channel_id=1, source_target_pairs={{1,0},{2,1},{3,2},{5,4},{6,5},{7,6},{9,8},{10,9},{11,10},{13,12},{... | collective-permute-start | bytes 270344 | tf_op jit(solution)/shard_map/ppermute | solution.py:878
  78.2 2.8 copy-start.4
  81.0 0.6 copy-start.5
  93.0 6.1 %collective-permute-start.11 = (f32[14,8,128]{2,1,0:T(8,128)S(1)}, f32[14,8,128]{2,1,0:T(8,128)S(1)}, u32[]{:S(2)}, u32[]{:S(2)}) collective-permute-start(f32[14,8,128]{2,1,0:T(8,128)S(1)} %get-tuple-element.137), channel_id=1, source_target_pairs={{4,0},{8,4},{12,8},{16,12},{20,16},{24,20},{28,24},{5,1},{9,5},{13... | collective-permute-start | bytes 172040 | tf_op jit(solution)/shard_map/ppermute | solution.py:871
  94.3 6.6 %collective-permute-start.10 = (f32[14,8,128]{2,1,0:T(8,128)S(1)}, f32[14,8,128]{2,1,0:T(8,128)S(1)}, u32[]{:S(2)}, u32[]{:S(2)}) collective-permute-start(f32[14,8,128]{2,1,0:T(8,128)S(1)} %get-tuple-element.138), channel_id=1, source_target_pairs={{0,4},{4,8},{8,12},{12,16},{16,20},{20,24},{24,28},{1,5},{5,9},{9,... | collective-permute-start | bytes 172040 | tf_op jit(solution)/shard_map/ppermute | solution.py:870
  99.1 55.3 %copy-start.2 = (f32[14,8,128]{2,1,0:T(8,128)}, f32[14,8,128]{2,1,0:T(8,128)S(1)}, u32[]{:S(2)}) copy-start(f32[14,8,128]{2,1,0:T(8,128)S(1)} %collective-permute-done.11.high_d) | copy-start | bytes 172036
  100.9 1.7 copy-start.3
  102.6 51.1 %collective-permute-start.12 = (f32[22,8,128]{2,1,0:T(8,128)}, f32[22,8,128]{2,1,0:T(8,128)}, u32[]{:S(2)}, u32[]{:S(2)}) collective-permute-start(f32[22,8,128]{2,1,0:T(8,128)} %bitcast.11), channel_id=1, source_target_pairs={{0,1},{1,2},{2,3},{4,5},{5,6},{6,7},{8,9},{9,10},{10,11},{12,13},{... | collective-permute-start | bytes 270344 | tf_op jit(solution)/shard_map/ppermute | solution.py:877
  106.9 46.9 %collective-permute-start.13 = (f32[22,8,128]{2,1,0:T(8,128)}, f32[22,8,128]{2,1,0:T(8,128)}, u32[]{:S(2)}, u32[]{:S(2)}) collective-permute-start(f32[22,8,128]{2,1,0:T(8,128)} %bitcast.12), channel_id=1, source_target_pairs={{1,0},{2,1},{3,2},{5,4},{6,5},{7,6},{9,8},{10,9},{11,10},{13,12},{... | collective-permute-start | bytes 270344 | tf_op jit(solution)/shard_map/ppermute | solution.py:878
  236.5 7.8 %collective-permute-start.14 = (f32[84,128]{1,0:T(8,128)}, f32[84,128]{1,0:T(8,128)S(1)}, u32[]{:S(2)}, u32[]{:S(2)}) collective-permute-start(f32[84,128]{1,0:T(8,128)} %get-tuple-element.102), channel_id=1, source_target_pairs={{0,28},{1,29},{2,30},{3,31},{4,0},{5,1},{6,2},{7,3},{8,4},{9,5},{1... | collective-permute-start | bytes 129032 | tf_op jit(solution)/shard_map/ppermute | solution.py:862
  240.6 3.8 collective-permute-start.15
  240.6 3.8 collective-permute-start.16
  244.3 0.6 copy-start.14
  244.3 0.6 copy-start.10
  244.3 0.6 copy-start.11
  255.6 8.7 %collective-permute-start.17 = (f32[84,128]{1,0:T(8,128)}, f32[84,128]{1,0:T(8,128)S(1)}, u32[]{:S(2)}, u32[]{:S(2)}) collective-permute-start(f32[84,128]{1,0:T(8,128)} %get-tuple-element.112), channel_id=1, source_target_pairs={{0,4},{1,5},{2,6},{3,7},{4,8},{5,9},{6,10},{7,11},{8,12},{9,13},{1... | collective-permute-start | bytes 129032 | tf_op jit(solution)/shard_map/ppermute | solution.py:862
  256.0 8.4 %collective-permute-start.18 = (f32[84,128]{1,0:T(8,128)}, f32[84,128]{1,0:T(8,128)S(1)}, u32[]{:S(2)}, u32[]{:S(2)}) collective-permute-start(f32[84,128]{1,0:T(8,128)} %get-tuple-element.113), channel_id=1, source_target_pairs={{0,1},{1,2},{2,3},{3,0},{4,5},{5,6},{6,7},{7,4},{8,9},{9,10},{10,1... | collective-permute-start | bytes 129032 | tf_op jit(solution)/shard_map/ppermute | solution.py:862
  256.9 7.4 %collective-permute-start.19 = (f32[63,128]{1,0:T(8,128)}, f32[63,128]{1,0:T(8,128)S(1)}, u32[]{:S(2)}, u32[]{:S(2)}) collective-permute-start(f32[63,128]{1,0:T(8,128)} %get-tuple-element.114), channel_id=1, source_target_pairs={{0,5},{1,6},{2,7},{3,4},{4,9},{5,10},{6,11},{7,8},{8,13},{9,14},{1... | collective-permute-start | bytes 96776 | tf_op jit(solution)/shard_map/ppermute | solution.py:862
  264.3 0.6 copy-start.15
  264.3 0.6 copy-start.6
  264.4 0.6 copy-start.7
Sparse Core Ops, SparseCore 0:
  278.7 139.0 all-reduce.9

commit v2 on v1

--- a/solution.py
+++ b/solution.py
@@ -621,9 +621,10 @@
 
 
 def head_kernel(
-    own, low_d, high_d, low_h, high_h, sums, conv1, head_w, head_b, voxels,
-    grown, slope_out, stats, d_head, d_rows,
+    own, low_d, high_d, low_h, high_h, all_sums, conv1, head_w, head_b, voxels,
+    grown, slope_out, stats, d_head, d_rows, sums,
 ):
+    sums[...] = jnp.sum(all_sums[...].reshape(-1, 8, WIDE), 0)
     grown_lines(own, low_d, high_d, low_h, high_h, grown)
     rows = 11 * 12 * 8
     both = grown[...].reshape(rows, WIDE)
@@ -727,6 +728,7 @@
     conv_weight_grad(side_own, own, 64, grads, 3)
     carry[...] = grads[0:24, :]
     flatten(grads, 20, GROUPS - CUTS[3], flat)
+    flat[3912:, :] = jnp.zeros((4096 - 3912, WIDE), F32)
     tap_weights_back(conv0, 3, weights)
     taps(act, 0, 9, 0, 8, side_own)
 
@@ -805,6 +807,7 @@
     put_hidden_rows(grads, 0, 1, colsum(d_hat * hat))
     put_hidden_rows(grads, 4, 1, colsum(d_hat))
     flatten(grads, 0, CUTS[1], flat)
+    flat[1176:, :] = jnp.zeros((8, WIDE), F32)
 
 
 def arr(*shape):
@@ -892,6 +895,21 @@
     return jnp.broadcast_to(ids[:, None], (ROWS, WIDE)), jnp.broadcast_to(ids[None], (8, ROWS))
 
 
+def exchanged_sum(value, axis, size):
+    step = 1
+    while step < size:
+        radix = 4 if size // step >= 4 else 2
+        got = [value]
+        for k in range(1, radix):
+            pairs = [(i, i ^ (k * step)) for i in range(size)]
+            got.append(lax.ppermute(value, axis, pairs))
+        while len(got) > 1:
+            got = [got[i] + got[i + 1] for i in range(0, len(got), 2)]
+        value = got[0]
+        step *= radix
+    return value
+
+
 def adamw(param, grad, first, second, scale):
     grad = grad * scale
     first = beta_one * first + (1.0 - beta_one) * grad
@@ -968,10 +986,11 @@
         name="conv",
     )
     near = beside(tok3, sizes)
-    stats = lax.psum(stats, both)
-    tok3, slope, tail, d_head, d_rows = call(
+    stats = lax.all_gather(stats, both, axis=0, tiled=True)
+    tok3, slope, tail, d_head, d_rows, stats = call(
         head_kernel,
-        [arr(11, 12, 8, WIDE), arr(11, 12, 8, WIDE), arr(8, WIDE), arr(WIDE, WIDE), arr(8, WIDE)],
+        [arr(11, 12, 8, WIDE), arr(11, 12, 8, WIDE), arr(8, WIDE), arr(WIDE, WIDE), arr(8, WIDE)]
+        + [arr(8, WIDE)],
         [],
         tok3, *near, stats, conv1, head_w, head_b, voxels,
         name="head",
@@ -979,10 +998,10 @@
     d_head = jnp.concatenate([d_head[:EMB, :CLASSES].reshape(-1), d_rows[2, :CLASSES]])
     d_head = jnp.pad(d_head, (0, 24 * EMB - CLASSES * (EMB + 1))).reshape(24, EMB)
     d_head = jnp.pad(d_head, ((0, 0), (0, WIDE - EMB)))
-    tail = lax.psum(tail, both)
+    tail = exchanged_sum(exchanged_sum(tail, "mp", rows), "slab", slabs)
     d_own, flat3, carry3 = call(
         conv_back_kernel,
-        [arr(PLANE, 8, WIDE), arr(3 * (CUTS[4] - CUTS[3]), WIDE), arr(24, WIDE)],
+        [arr(PLANE, 8, WIDE), arr(4096, WIDE), arr(24, WIDE)],
         [
             pltpu.VMEM((5236, WIDE), F32),
             pltpu.VMEM((11, 12, 8, WIDE), F32),
@@ -994,7 +1013,8 @@
         ends, tok3, slope, tail, grown, pre, conv0, conv1, d_rows, d_head,
         name="conv_back",
     )
-    flat3 = lax.psum(flat3.reshape(-1), both)
+    flat3 = lax.psum_scatter(flat3, both, scatter_dimension=0, tiled=True)
+    flat3 = lax.all_gather(flat3, both, axis=0, tiled=True)
     d_mid, grads1, flat2, carry2, *parts = call(
         back_two_kernel,
         [SQUARE, arr(1168, WIDE), arr(3 * (CUTS[3] - CUTS[2]), WIDE), arr(32, WIDE)] + PARTS,
@@ -1002,7 +1022,7 @@
         d_own, carry3, lay1, lay2, tok2, save2, lse2, mixed2, mid2, hpre2, mid1, hpre1,
         name="back_two",
     )
-    flat2 = lax.psum(flat2.reshape(-1), both)
+    flat2 = lax.psum(flat2, both)
     parts = passed(parts, -1, sizes)
     d_window, flat1, carry1, *parts = call(
         back_shifted_kernel,
@@ -1011,18 +1031,21 @@
         d_mid, *parts, lay1, *region, window, save1, lse1, mixed1, grads1, carry2,
         name="back_shifted",
     )
-    flat1 = lax.psum(flat1.reshape(-1), both)
+    flat1 = lax.psum(flat1, both)
     parts = passed(parts, 1, sizes)
     (flat0,) = call(
         back_first_kernel,
-        [arr(3 * (CUTS[1] - CUTS[0]), WIDE)],
+        [arr(1184, WIDE)],
         [pltpu.VMEM((1572, WIDE), F32), pltpu.VMEM((ROWS, WIDE), F32)] + BACKWARD,
         d_mid, d_window, *parts, tok1, lay0, lay1, merge, dense, tok0, save0, lse0, mixed0, mid0,
         hpre0, carry1,
         name="back_first",
     )
-    flat0 = lax.psum(flat0.reshape(-1), both)
-    gradient = jnp.concatenate([flat0, flat1, flat2, flat3])[:NPARAM]
+    flat0 = lax.psum_scatter(flat0, "mp", scatter_dimension=0, tiled=True)
+    flat0 = lax.psum(flat0, "slab")
+    flat0 = lax.all_gather(flat0, "mp", axis=0, tiled=True)
+    gradient = jnp.concatenate([flat0[:1176], flat1, flat2, flat3[:3912]], 0)
+    gradient = gradient.reshape(-1)[:NPARAM]
     grad_norm = jnp.sqrt(jnp.sum(gradient * gradient))
     scale = jnp.minimum(1.0, clip_norm / (grad_norm + 1e-06))
     new_params, new_first, new_second = adamw(params, gradient, moment_one, moment_two, scale)

time: 447 us -> 699 us (1.56)
  waiting for transfers between devices: 160 us -> 435 us
  blocking collectives: 82.8 us -> 54.7 us
    reduce_scatter x0 -> x1, waiting for transfers between devices: none -> 140 us  [on_device(): flat3 = lax.psum_scatter(flat3, both, scatter_dimension=0, tiled=True)]
    psum x2 -> x0, blocking collectives: 82.8 us -> none  [the longest x1 41.9 us: on_device(): stats = lax.psum(stats, both)]
    psum x1 -> x2, waiting for transfers between devices: 137 us -> 197 us  [the longest x1 131 us: on_device(): flat2 = lax.psum(flat2, both)]
    all_gather x0 -> x2, blocking collectives: none -> 54.7 us  [the longest x1 46.9 us: on_device(): stats = lax.all_gather(stats, both, axis=0, tiled=True)]
    all_gather x0 -> x1, waiting for transfers between devices: none -> 50.4 us  [on_device(): flat3 = lax.all_gather(flat3, both, axis=0, tiled=True)]
    unnamed x1 -> x6, waiting for transfers between devices: 0.02 us -> 19.5 us
  transfers between devices with their start and end apart: 21 -> 32, of which waited for: 10 -> 18; matrix products, arithmetic and copies ran while one was open for 2% -> 2% of each run, Pallas kernels for 0% -> 0%
where the time goes in v2:
time: 699 us; the launch traced here: 691 us
  waiting for transfers between devices  435 us (62%)
  Pallas kernels  105 us (15%)
  blocking collectives  54.7 us (8%)
  starting transfers between devices  42.4 us (6%)
  local copies, waits for them, and re-layouts  22 us (3%)
  between operations  16.4 us (2%)
  other arithmetic  15.8 us (2%)
    reduce_scatter x1, waiting for transfers between devices, on_device(): flat3 = lax.psum_scatter(flat3, both, scatter_dimension=0, tiled=True)  140 us
    psum x1, waiting for transfers between devices, on_device(): flat2 = lax.psum(flat2, both)  131 us
    pallas_call x10, Pallas kernels, call(): pl.pallas_call(kernel, out_shape=list(outs), in_specs=specs, out_specs=[v...  105 us
    psum x1, waiting for transfers between devices, on_device(): flat0 = lax.psum(flat0, 'slab')  65.9 us
    all_gather x1, waiting for transfers between devices, on_device(): flat3 = lax.all_gather(flat3, both, axis=0, tiled=True)  50.4 us
    all_gather x1, blocking collectives, on_device(): stats = lax.all_gather(stats, both, axis=0, tiled=True)  46.9 us
    unnamed x6, waiting for transfers between devices  19.5 us
    ppermute x12, waiting for transfers between devices, passed(): moved.append(lax.ppermute(part, ('slab', 'mp'), pairs))  17.2 us
  transfers between devices with their start and end apart: 32, of which 18 were waited for; matrix products, arithmetic and copies ran while one was open for 2% of the time, Pallas kernels for 0%

profile of v2, /device:TPU:0, one launch (start us, length us, event | category | flops | bytes accessed | tf_op | source)
XLA Modules:
  0.0 691.5 jit_solution(13789943015339523897)
XLA Ops:
  7.2 4.0 pad_bitcast_fusion.flat
  11.2 4.7 prep.1
  15.8 9.5 %first.1 = (f32[384,384]{1,0:T(8,128)}, f32[384,128]{1,0:T(8,128)}, f32[384,384]{1,0:T(8,128)}, f32[384,128]{1,0:T(8,128)}, f32[384,128]{1,0:T(8,128)}, /*index=...) custom-call(f32[49,7,384]{2,1,0:T(8,128)} %bitcast.24, ...), custom_call_target="tpu_custom_call" | custom-call | tf_op jit(solution)/shard_map/first/pallas_call | solution.py:821
  25.3 6.4 collective-permute-start.2
  33.6 2.3 collective-permute-done.pa
  37.4 7.4 %shifted.1 = (f32[384,128]{1,0:T(8,128)}, f32[384,384]{1,0:T(8,128)}, f32[384,128]{1,0:T(8,128)}, f32[384,128]{1,0:T(8,128)}, f32[384,128]{1,0:T(8,128)}, /*inde...) custom-call(f32[384,128]{1,0:T(8,128)} %get-tuple-element.71.own, f32[84,128]{1,0:T(8,128)} %copy-done.8, ...), custom_call_target="tpu_custom_call" | custom-call | tf_op jit(solution)/shard_map/shifted/pallas_call | solution.py:821
  45.5 6.5 collective-permute-done.5.qc
  52.9 9.5 %second.1 = (f32[384,128]{1,0:T(8,128)}, f32[384,384]{1,0:T(8,128)}, f32[384,128]{1,0:T(8,128)}, f32[384,384]{1,0:T(8,128)}, f32[384,128]{1,0:T(8,128)}, /*index...) custom-call(f32[384,128]{1,0:T(8,128)} %get-tuple-element.70.tok1, ...), custom_call_target="tpu_custom_call" | custom-call | tf_op jit(solution)/shard_map/second/pallas_call | solution.py:821
  63.3 1.3 collective-permute-start.7
  64.6 4.5 collective-permute-start.6
  70.9 1.0 pad_maximum_fusion
  71.9 1.3 collective-permute-start.8
  73.2 1.5 collective-permute-start.9
  75.3 2.8 collective-permute-done.9.high_h
  78.8 10.5 %conv.1 = (f32[11,12,8,128]{3,2,1,0:T(8,128)}, f32[9,10,8,128]{3,2,1,0:T(8,128)}, f32[49,8,128]{2,1,0:T(8,128)}, f32[8,128]{1,0:T(8,128)}) custom-call(s32[4]{0:T(128)} %add_convert_fusion.1.ends, f32[49,8,128]{2,1,0:T(8,128)} %get-tuple-element.80.own, f32[14,8,128]{2,1,0:T(8,128)} %copy-done.1, f32[14,8,128]{2,1,0:T(8,128)} %copy-done, ...), custom_call_target="tpu_custom_call" | custom-call | tf_op jit(solution)/shard_map/conv/pallas_call | solution.py:821
  90.2 1.3 collective-permute-start.11
  91.4 4.9 collective-permute-start.10
  96.6 1.6 collective-permute-done.10.low_d
  99.1 4.2 collective-permute-start.12
  103.4 1.3 collective-permute-start.13
  107.0 46.9 %all_gather.9.all_sums = f32[256,128]{1,0:T(8,128)} all-gather(f32[8,128]{1,0:T(8,128)} %get-tuple-element.84), channel_id=1, replica_groups=mesh['slab'=8,'mp'=4] {'slab','mp'}, dimensions={0}, use_global_device_ids=true | all-gather | bytes 135168 | tf_op jit(solution)/shard_map/all_gather | solution.py:989
  154.6 3.6 head.1
  158.3 2.0 collective-permute-start.15
  160.2 1.3 collective-permute-done.16
  162.8 3.5 collective-permute-start.17
  168.8 3.7 collective-permute-done.20
  173.1 21.3 %conv_back.1 = (f32[49,8,128]{2,1,0:T(8,128)}, f32[4096,128]{1,0:T(8,128)}, f32[24,128]{1,0:T(8,128)}) custom-call(s32[4]{0:T(128)} %add_convert_fusion.1.ends, f32[11,12,8,128]{3,2,1,0:T(8,128)} %get-tuple-element.87.tok, f32[11,12,8,128]{3,2,1,0:T(8,128)} %get-tuple-element.88.slope, f32[8,128]{1,0:T(8,128)} %add.180.sums, ...), custom_call_target="tpu_custom_call" | custom-call | tf_op jit(solution)/shard_map/conv_back/pallas_call | solution.py:821
  194.4 14.2 %back_two.1 = (f32[384,128]{1,0:T(8,128)}, f32[1168,128]{1,0:T(8,128)}, f32[864,128]{1,0:T(8,128)}, f32[32,128]{1,0:T(8,128)}, f32[84,128]{1,0:T(8,128)}, /*index=5*/f32[84,128]{1,0:T(8,128)}, f32[63,128]{1,0:T(8,128)}) custom-call(f32[49,8,128]{2,1,0:T(8,128)} %get-tuple-element.93.d_own, f32[24,128]{1,0:T(8,128)} %get-tuple-element.94.carry, ...), custom_call_target="tpu_custom_call" | custom-call | tf_op jit(solution)/shard_map/back_two/pallas_call | solution.py:821
  209.6 1.9 collective-permute-start.23
  211.5 1.9 collective-permute-done.23.pc
  214.1 10.7 %back_shifted.1 = (f32[384,128]{1,0:T(8,128)}, f32[888,128]{1,0:T(8,128)}, f32[16,128]{1,0:T(8,128)}, f32[84,128]{1,0:T(8,128)}, f32[84,128]{1,0:T(8,128)}, /*index=5*/f32[63,128]{1,0:T(8,128)}) custom-call(f32[384,128]{1,0:T(8,128)} %get-tuple-element.103.own.d_mid, f32[84,128]{1,0:T(8,128)} %copy-done.10, f32[84,128]{1,0:T(8,128)} %copy-done.11, ...), custom_call_target="tpu_custom_call" | custom-call | tf_op jit(solution)/shard_map/back_shifted/pallas_call | solution.py:821
  224.7 2.5 collective-permute-start.24
  227.3 1.2 collective-permute-start.25
  228.5 1.6 collective-permute-start.26
  230.1 5.6 collective-permute-done.26.qc
  236.4 13.6 %back_first.1 = f32[1184,128]{1,0:T(8,128)} custom-call(f32[384,128]{1,0:T(8,128)} %get-tuple-element.103.own.d_mid, f32[384,128]{1,0:T(8,128)} %get-tuple-element.113.own, f32[84,128]{1,0:T(8,128)} %copy-done.14, f32[84,128]{1,0:T(8,128)} %copy-done.15, f32[63,128]{1,0:T(8,128)} %copy-done.17, f32[384,128]{1,0:T(8,128)} %get-tuple-element.70.tok1, ...), custom_call_target="tpu_custom_call" | custom-call | tf_op jit(solution)/shard_map/back_first/pallas_call | solution.py:821
  250.9 18.2 %reduce-scatter.7.cloned.1.call-done = f32[296,128]{1,0:T(8,128)} async-done(((f32[1184,128]{1,0:T(8,128)}), f32[296,128]{1,0:T(8,128)}) %reduce-scatter.7.cloned.1.call-update) | async-done | bytes 151568
  269.1 139.6 %reduce-scatter.5.cloned.1.call-done = f32[128,128]{1,0:T(8,128)} async-done(((f32[4096,128]{1,0:T(8,128)}), f32[128,128]{1,0:T(8,128)}) %reduce-scatter.5.cloned.1.call-update) | async-done | bytes 65552 | tf_op jit(solution)/shard_map/reduce_scatter | solution.py:1016
  409.4 1.2 slice.65
  410.6 1.2 slice.64
  411.8 65.9 %all-reduce.12.cloned.1.call-done = f32[296,128]{1,0:T(8,128)} async-done(((f32[296,128]{1,0:T(8,128)}), f32[296,128]{1,0:T(8,128)}) %all-reduce.12.cloned.1.call-update) | async-done | bytes 151568 | tf_op jit(solution)/shard_map/psum | solution.py:1045
  477.7 7.8 %all_gather.10 = f32[1184,128]{1,0:T(8,128)S(1)} all-gather(f32[296,128]{1,0:T(8,128)} %all-reduce.12.cloned.1.call-done), channel_id=1, replica_groups=mesh['slab'=8,'mp'=4] {'mp'}, dimensions={0}, use_global_device_ids=true | all-gather | bytes 757760 | tf_op jit(solution)/shard_map/all_gather | solution.py:1046
  486.3 50.4 %all-gather.2.cloned.1.call-done = f32[4096,128]{1,0:T(8,128)} async-done(((f32[128,128]{1,0:T(8,128)}), f32[4096,128]{1,0:T(8,128)}) %all-gather.2.cloned.1.call-update) | async-done | bytes 2097168 | tf_op jit(solution)/shard_map/all_gather | solution.py:1017
  536.7 3.0 slice.76
  539.7 131.4 %all-reduce.14.cloned.1.call-done = (f32[864,128]{1,0:T(8,128)}, f32[888,128]{1,0:T(8,128)}) async-done(((f32[864,128]{1,0:T(8,128)}, f32[888,128]{1,0:T(8,128)}), (f32[864,128]{1,0:T(8,128)}, f32[888,128]{1,0:T(8,128)})) %all-reduce.14.cloned.1.call-update) | async-done | bytes 897040 | tf_op jit(solution)/shard_map/psum | solution.py:1025
  671.1 2.2 maximum_bitcast_fusion
  673.2 1.5 multiply_reduce_fusion
  675.5 7.9 %multiply_subtract_fusion = (f32[872558]{0:T(1024)}, f32[872558]{0:T(1024)}, f32[872558]{0:T(1024)}) fusion(f32[872558]{0:T(1024)} %param.9, f32[]{:T(128)S(6)} %min_shard_map.3, f32[875520]{0:T(1024)S(1)} %maximum_bitcast_fusion, f32[872558]{0:T(1024)} %param.10, f32[872558]{0:T(1024)} %param.11), kind=kLoop, calls=%fused_computation.4 | loop fusion | flops 13960928 | bytes 24431628 | tf_op jit(solution)/shard_map/sub | solution.py:919
  (119 shorter events, 22.7 us)
Async XLA Ops:
  7.2 261.9 %reduce-scatter.7.cloned.1.call-start = ((), (), s32[]{:S(2)}) async-start(), calls=%async_computation.5 | async-start | bytes 757760
  11.2 34.3 %copy-start.20 = (s32[7,7,7]{2,1,0:T(8,128)S(1)}, s32[7,7,7]{2,1,0:T(8,128)}, u32[]{:S(2)}) copy-start(s32[7,7,7]{2,1,0:T(8,128)} %param.8) | copy-start | bytes 4120
  15.8 53.3 %copy-start.21 = (s32[7,7,7]{2,1,0:T(8,128)S(1)}, s32[7,7,7]{2,1,0:T(8,128)}, u32[]{:S(2)}) copy-start(s32[7,7,7]{2,1,0:T(8,128)} %param.7) | copy-start | bytes 4120
  25.3 8.3 %collective-permute-start.2 = (f32[63,128]{1,0:T(8,128)}, f32[63,128]{1,0:T(8,128)S(1)}, u32[]{:S(2)}, u32[]{:S(2)}) collective-permute-start(f32[63,128]{1,0:T(8,128)} %get-tuple-element.74), channel_id=1, source_target_pairs={{0,31},{1,28},{2,29},{3,30},{4,3},{5,0},{6,1},{7,2},{8,7},{9,4},{1... | collective-permute-start | bytes 96776 | tf_op jit(solution)/shard_map/ppermute | solution.py:865
  31.7 4.3 collective-permute-start
  32.3 3.7 collective-permute-start.1
  33.6 3.8 copy-start.18
  36.0 1.4 copy-start.8
  36.0 1.4 copy-start.9
  44.8 7.1 %collective-permute-start.5 = (f32[63,128]{1,0:T(8,128)}, f32[63,128]{1,0:T(8,128)S(1)}, u32[]{:S(2)}, u32[]{:S(2)}) collective-permute-start(f32[63,128]{1,0:T(8,128)} %get-tuple-element.78), channel_id=1, source_target_pairs={{0,5},{1,6},{2,7},{3,4},{4,9},{5,10},{6,11},{7,8},{8,13},{9,14},{1... | collective-permute-start | bytes 96776 | tf_op jit(solution)/shard_map/ppermute | solution.py:865
  45.3 7.0 %collective-permute-start.3 = (f32[84,128]{1,0:T(8,128)}, f32[84,128]{1,0:T(8,128)S(1)}, u32[]{:S(2)}, u32[]{:S(2)}) collective-permute-start(f32[84,128]{1,0:T(8,128)} %get-tuple-element.76), channel_id=1, source_target_pairs={{0,4},{1,5},{2,6},{3,7},{4,8},{5,9},{6,10},{7,11},{8,12},{9,13},{1... | collective-permute-start | bytes 129032 | tf_op jit(solution)/shard_map/ppermute | solution.py:865
  45.3 7.0 %collective-permute-start.4 = (f32[84,128]{1,0:T(8,128)}, f32[84,128]{1,0:T(8,128)S(1)}, u32[]{:S(2)}, u32[]{:S(2)}) collective-permute-start(f32[84,128]{1,0:T(8,128)} %get-tuple-element.77), channel_id=1, source_target_pairs={{0,1},{1,2},{2,3},{3,0},{4,5},{5,6},{6,7},{7,4},{8,9},{9,10},{10,1... | collective-permute-start | bytes 129032 | tf_op jit(solution)/shard_map/ppermute | solution.py:865
  52.3 0.6 copy-start.13
  63.3 6.7 collective-permute-start.7
  64.6 6.4 collective-permute-start.6
  70.0 8.1 %copy-start = (f32[14,8,128]{2,1,0:T(8,128)}, f32[14,8,128]{2,1,0:T(8,128)S(1)}, u32[]{:S(2)}) copy-start(f32[14,8,128]{2,1,0:T(8,128)S(1)} %collective-permute-done.7.high_d) | copy-start | bytes 172036
  70.9 7.2 %copy-start.1 = (f32[14,8,128]{2,1,0:T(8,128)}, f32[14,8,128]{2,1,0:T(8,128)S(1)}, u32[]{:S(2)}) copy-start(f32[14,8,128]{2,1,0:T(8,128)S(1)} %collective-permute-done.6.low_d) | copy-start | bytes 172036
  71.9 3.4 collective-permute-start.8
  73.2 4.9 collective-permute-start.9
  75.3 2.8 copy-start.6
  78.1 0.6 copy-start.7
  90.2 6.4 collective-permute-start.11
  91.4 6.7 collective-permute-start.10
  96.6 58.0 %copy-start.2 = (f32[14,8,128]{2,1,0:T(8,128)}, f32[14,8,128]{2,1,0:T(8,128)S(1)}, u32[]{:S(2)}) copy-start(f32[14,8,128]{2,1,0:T(8,128)S(1)} %collective-permute-done.11.high_d) | copy-start | bytes 172036
  98.2 56.4 %copy-start.3 = (f32[14,8,128]{2,1,0:T(8,128)}, f32[14,8,128]{2,1,0:T(8,128)S(1)}, u32[]{:S(2)}) copy-start(f32[14,8,128]{2,1,0:T(8,128)S(1)} %collective-permute-done.10.low_d) | copy-start | bytes 172036
  99.1 54.8 %collective-permute-start.12 = (f32[22,8,128]{2,1,0:T(8,128)S(1)}, f32[22,8,128]{2,1,0:T(8,128)S(1)}, u32[]{:S(2)}, u32[]{:S(2)}) collective-permute-start(f32[22,8,128]{2,1,0:T(8,128)S(1)} %bitcast.26), channel_id=1, source_target_pairs={{0,1},{1,2},{2,3},{4,5},{5,6},{6,7},{8,9},{9,10},{10,11},{12,13},{... | collective-permute-start | bytes 270344 | tf_op jit(solution)/shard_map/ppermute | solution.py:880
  103.4 50.6 %collective-permute-start.13 = (f32[22,8,128]{2,1,0:T(8,128)S(1)}, f32[22,8,128]{2,1,0:T(8,128)S(1)}, u32[]{:S(2)}, u32[]{:S(2)}) collective-permute-start(f32[22,8,128]{2,1,0:T(8,128)S(1)} %bitcast.25), channel_id=1, source_target_pairs={{1,0},{2,1},{3,2},{5,4},{6,5},{7,6},{9,8},{10,9},{11,10},{13,12},{... | collective-permute-start | bytes 270344 | tf_op jit(solution)/shard_map/ppermute | solution.py:881
  153.9 0.7 copy-start.4
  154.0 0.7 copy-start.5
  158.2 3.2 collective-permute-start.16
  158.3 3.9 collective-permute-start.15
  160.2 1.9 collective-permute-start.14
  162.8 5.1 collective-permute-start.19
  162.8 5.1 collective-permute-start.18
  162.8 5.1 collective-permute-start.17
  168.0 4.6 collective-permute-start.20
  208.7 4.8 collective-permute-start.21
  209.5 3.9 collective-permute-start.22
  209.6 3.9 collective-permute-start.23
  213.4 0.7 copy-start.11
  224.7 11.0 %collective-permute-start.24 = (f32[84,128]{1,0:T(8,128)}, f32[84,128]{1,0:T(8,128)S(1)}, u32[]{:S(2)}, u32[]{:S(2)}) collective-permute-start(f32[84,128]{1,0:T(8,128)} %get-tuple-element.114), channel_id=1, source_target_pairs={{0,4},{1,5},{2,6},{3,7},{4,8},{5,9},{6,10},{7,11},{8,12},{9,13},{1... | collective-permute-start | bytes 129032 | tf_op jit(solution)/shard_map/ppermute | solution.py:865
  227.3 8.5 %collective-permute-start.25 = (f32[84,128]{1,0:T(8,128)}, f32[84,128]{1,0:T(8,128)S(1)}, u32[]{:S(2)}, u32[]{:S(2)}) collective-permute-start(f32[84,128]{1,0:T(8,128)} %get-tuple-element.115), channel_id=1, source_target_pairs={{0,1},{1,2},{2,3},{3,0},{4,5},{5,6},{6,7},{7,4},{8,9},{9,10},{10,1... | collective-permute-start | bytes 129032 | tf_op jit(solution)/shard_map/ppermute | solution.py:865
  228.5 7.3 %collective-permute-start.26 = (f32[63,128]{1,0:T(8,128)}, f32[63,128]{1,0:T(8,128)S(1)}, u32[]{:S(2)}, u32[]{:S(2)}) collective-permute-start(f32[63,128]{1,0:T(8,128)} %get-tuple-element.116), channel_id=1, source_target_pairs={{0,5},{1,6},{2,7},{3,4},{4,9},{5,10},{6,11},{7,8},{8,13},{9,14},{1... | collective-permute-start | bytes 96776 | tf_op jit(solution)/shard_map/ppermute | solution.py:865
  235.8 0.6 copy-start.15
  250.1 158.7 %reduce-scatter.5.cloned.1.call-start = ((), (), s32[]{:S(2)}) async-start(), calls=%async_computation.3 | async-start | bytes 2162688 | tf_op jit(solution)/shard_map/reduce_scatter | solution.py:1016
  250.8 226.9 %all-reduce.12.cloned.1.call-start = ((), (), s32[]{:S(2)}) async-start(), calls=%async_computation.2 | async-start | bytes 303104 | tf_op jit(solution)/shard_map/psum | solution.py:1045
  269.1 267.6 %all-gather.2.cloned.1.call-start = ((), (), s32[]{:S(2)}) async-start(), calls=%async_computation.4 | async-start | bytes 2162688 | tf_op jit(solution)/shard_map/all_gather | solution.py:1017
  408.8 262.3 %all-reduce.14.cloned.1.call-start = ((), (), s32[]{:S(2)}) async-start(), calls=%async_computation.6 | async-start | bytes 1794048 | tf_op jit(solution)/shard_map/psum | solution.py:1025
  (6 other events, 3.7 us)
Sparse Core Ops, SparseCore 0:
  250.2 18.8 reduce-scatter.6
  271.9 136.8 reduce-scatter.4
  412.5 65.1 all-reduce.11
  480.4 56.2 all-gather.1
  542.4 128.6 all-reduce.13
